TPU v7x, 128 devices: a whole 4x4x4 slice. The times are simulated.
128 devices in a mesh: ctx: 64 (over z_hi, x, y, core), fsdp: 2 (over z_lo).
Axes of the slice: x: 4, y: 4, z: 4 (z_hi: 2, z_lo: 2; z = z_hi * 2 + z_lo), core: 2. Of those that a mesh axis runs over, the one named last changes fastest.
Arguments:
- layer_in: bfloat16 [16384, 960], P(('ctx', 'fsdp')), may hold values from -6 to 6
- attn_gain: bfloat16 [960], P('ctx'), may hold values from 0.5 to 1.5
- query_weight: bfloat16 [960, 960], P('ctx', 'fsdp'), may hold values from -0.1875 to 0.1875
- key_weight: bfloat16 [960, 320], P('ctx', 'fsdp'), may hold values from -0.1875 to 0.1875
- value_weight: bfloat16 [960, 320], P('ctx', 'fsdp'), may hold values from -0.1875 to 0.1875
- output_weight: bfloat16 [960, 960], P('ctx', 'fsdp'), may hold values from -1.5 to 1.5
- ffn_gain: bfloat16 [960], P('ctx'), may hold values from 0.5 to 1.5
- gate_weight: bfloat16 [960, 2560], P('ctx', 'fsdp'), may hold values from -0.1875 to 0.1875
- up_weight: bfloat16 [960, 2560], P('ctx', 'fsdp'), may hold values from -0.1875 to 0.1875
- down_weight: bfloat16 [2560, 960], P('ctx', 'fsdp'), may hold values from -0.125 to 0.125
- out_cotangent: bfloat16 [16384, 960], P(('ctx', 'fsdp')), may hold values from -6 to 6
Outputs:
- layer_out: bfloat16 [16384, 960], P(('ctx', 'fsdp'))
- input_grad: float32 [16384, 960], P(('ctx', 'fsdp'))
- attn_gain_grad: float32 [960], P('ctx')
- query_grad: float32 [960, 960], P('ctx', 'fsdp')
- key_grad: float32 [960, 320], P('ctx', 'fsdp')
- value_grad: float32 [960, 320], P('ctx', 'fsdp')
- output_grad: float32 [960, 960], P('ctx', 'fsdp')
- ffn_gain_grad: float32 [960], P('ctx')
- gate_grad: float32 [960, 2560], P('ctx', 'fsdp')
- up_grad: float32 [960, 2560], P('ctx', 'fsdp')
- down_grad: float32 [2560, 960], P('ctx', 'fsdp')
All inputs are finite; a program needn't handle non-finite values.
Results may differ from a plain program's by a relative error of at most 0.04.
Values may be sent and summed in bfloat16 or wider, within the bound.
A program may use at most 448 MiB of HBM per device.

v0:
```python
import jax
import jax.numpy as jnp
from jax import lax
from jax.sharding import PartitionSpec as P

QH = 15
KEY_HEADS = 5
HEAD_SIZE = 64
QW = 960
KW = 320


EPS = 1e-05
ROPE_BASE = 10000.0
NEGATIVE = -1e30


def side_by_side(arrays, axis, dim, along):
    columns = [a.reshape(*a.shape[:along], -1) for a in arrays]
    both = jnp.concatenate(columns, axis=along)
    out, at, gathered = (lax.all_gather(both, axis, axis=dim, tiled=True), 0, [])
    for a, column in zip(arrays, columns):
        share = out[..., at : at + column.shape[along]]
        gathered.append(share.reshape(*share.shape[:along], *a.shape[along:]))
        at += column.shape[along]
    return tuple(gathered)


def in_one_piece(arrays, axis, dim, along):
    widths = [a.shape[along] for a in arrays]
    both = jnp.concatenate(arrays, axis=along)
    out = lax.all_gather(both, axis, axis=dim, tiled=True)
    return tuple(jnp.split(out, [sum(widths[:k]) for k in range(1, len(widths))], axis=along))


def in_blocks(x, dim, count):
    before, after = (x.shape[:dim], x.shape[dim + 1 :])
    return jnp.moveaxis(x.reshape(*before, count, -1, *after), dim, 0)


def summed_on_arrival(x, axis, dim):
    count = lax.axis_size(axis)
    parts = lax.all_to_all(in_blocks(x, dim, count), axis, 0, 0, tiled=True)
    return jnp.sum(parts.astype(jnp.float32), axis=0)


def sent_together(arrays, axis, dim, along):
    both = jnp.concatenate(arrays, axis=along)
    out, at, gathered = (summed_on_arrival(both, axis, dim), 0, [])
    for a in arrays:
        gathered.append(lax.slice_in_dim(out, at, at + a.shape[along], axis=along))
        at += a.shape[along]
    return tuple(gathered)


def sum_packed(arrays, axis, dims):
    count = lax.axis_size(axis)
    parts = [in_blocks(a, dim, count) for a, dim in zip(arrays, dims)]
    lines = jnp.concatenate([b.reshape(count, -1) for b in parts], axis=1)
    width = max(16, -(-lines.shape[1] // 1024) * 8)
    lines = jnp.pad(lines, ((0, 0), (0, width * 128 - lines.shape[1]))).reshape(-1, 128)
    flat, at, gathered = (lax.psum_scatter(lines, axis, tiled=True).reshape(-1), 0, [])
    for b in parts:
        part = b[0]
        gathered.append(flat[at : at + part.size].reshape(part.shape))
        at += part.size
    return tuple(gathered)


def contract_product(form, left, right):
    return jnp.einsum(form, left, right, preferred_element_type=jnp.float32)


def rotary_tables(positions):
    half = HEAD_SIZE // 2
    freq = ROPE_BASE ** (-(jnp.arange(half, dtype=jnp.float32) * 2.0 / HEAD_SIZE))
    angle = positions.astype(jnp.float32)[:, None] * freq[None, :]
    return (jnp.cos(angle)[:, None, :], jnp.sin(angle)[:, None, :])


def rotate(values, cosine, sine):
    count = values.shape[0]
    half = HEAD_SIZE // 2
    heads = values.reshape(count, -1, HEAD_SIZE)
    first = heads[..., :half]
    second = heads[..., half:]
    return jnp.concatenate(
        [first * cosine - second * sine, second * cosine + first * sine], -1
    ).reshape(count, -1)


def rotate_back(grads, cosine, sine):
    count = grads.shape[0]
    half = HEAD_SIZE // 2
    heads = grads.reshape(count, -1, HEAD_SIZE)
    first = heads[..., :half]
    second = heads[..., half:]
    return jnp.concatenate(
        [first * cosine + second * sine, second * cosine - first * sine], -1
    ).reshape(count, -1)


def normalize(hidden, gain):
    factor = lax.rsqrt(jnp.mean(hidden * hidden, -1, keepdims=True) + EPS)
    return (hidden * factor * gain, factor)


def normalize_back(hidden, factor, gain, grad):
    weighted = gain * grad
    back = factor * weighted - hidden * factor**3 * jnp.mean(weighted * hidden, -1, keepdims=True)
    return (back, jnp.sum(grad * hidden * factor, 0))


def local(
    layer_in,
    attn_gain,
    query_weight,
    key_weight,
    value_weight,
    output_weight,
    ffn_gain,
    gate_weight,
    up_weight,
    down_weight,
    out_cotangent,
):
    rows = layer_in.shape[0]
    pair = lax.axis_size("fsdp")
    cycle = lax.axis_size("ctx")
    cycle_pos = lax.axis_index("ctx")
    pair_pos = lax.axis_index("fsdp")
    block = rows * pair
    first_row = (cycle_pos * pair + pair_pos) * rows
    last_query = first_row + rows - 1
    groups = QH // KEY_HEADS
    score_scale = HEAD_SIZE ** (-0.5)
    gathered = (
        lax.all_gather(attn_gain, "ctx", axis=0, tiled=True),
        *side_by_side(
            (
                ffn_gain,
                query_weight,
                key_weight,
                value_weight,
                output_weight,
                gate_weight,
                up_weight,
            ),
            "ctx",
            0,
            1,
        ),
        lax.all_gather(down_weight, "ctx", axis=0, tiled=True),
    )
    gain_one = gathered[0].astype(jnp.float32)
    gain_two = gathered[1].astype(jnp.float32)
    mats = (
        lax.all_gather(gathered[2], "fsdp", axis=1, tiled=True),
        *in_one_piece((gathered[3], gathered[4]), "fsdp", 1, 0),
        lax.all_gather(gathered[5], "fsdp", axis=1, tiled=True),
        *in_one_piece((gathered[6], gathered[7]), "fsdp", 1, 0),
        lax.all_gather(gathered[8], "fsdp", axis=1, tiled=True),
    )
    w_query, w_key, w_value, w_output, w_gate, w_upward, w_down = mats
    positions = first_row + jnp.arange(rows, dtype=jnp.int32)
    cosine, sine = rotary_tables(positions)
    hidden = layer_in.astype(jnp.float32)
    normed_f, factor_one = normalize(hidden, gain_one)
    normed = normed_f.astype(jnp.bfloat16)
    query_pre = jnp.dot(normed, w_query, preferred_element_type=jnp.float32)
    key_pre = jnp.dot(normed, w_key, preferred_element_type=jnp.float32)
    value_pre = jnp.dot(normed, w_value, preferred_element_type=jnp.float32)
    query_rot = rotate(query_pre, cosine, sine).astype(jnp.bfloat16)
    key_rot = rotate(key_pre, cosine, sine).astype(jnp.bfloat16)
    value_low = value_pre.astype(jnp.bfloat16)
    key_block, value_block = in_one_piece((key_rot, value_low), "fsdp", 0, 1)
    query_head_rows = query_rot.reshape(rows, KEY_HEADS, groups, HEAD_SIZE)

    def scores_of(key_piece):
        key_head_rows = key_piece.reshape(-1, KEY_HEADS, HEAD_SIZE)
        attention_logits = (
            contract_product("amxb,jmb->mxaj", query_head_rows, key_head_rows) * score_scale
        )
        key_pos = jnp.arange(key_piece.shape[0], dtype=jnp.int32)
        mask = positions[:, None] >= key_pos[None, :]
        return (attention_logits, mask)

    initial = (
        jnp.full((KEY_HEADS, groups, rows), NEGATIVE, jnp.float32),
        jnp.zeros((KEY_HEADS, groups, rows), jnp.float32),
        jnp.zeros((rows, KEY_HEADS, groups, HEAD_SIZE), jnp.float32),
    )
    pieces = in_one_piece((key_block, value_block), "ctx", 0, 1)
    key_piece = pieces[0]
    value_portion = pieces[1]
    start = jnp.int32(0)

    def attend_compute(current):
        peak, total, accum = current
        attention_logits, mask = scores_of(key_piece)
        new_peak = jnp.maximum(peak, jnp.max(jnp.where(mask, attention_logits, NEGATIVE), -1))
        weight_tensors = jnp.where(mask, jnp.exp(attention_logits - new_peak[..., None]), 0.0)
        factor = jnp.exp(peak - new_peak)
        total = jnp.sum(weight_tensors, -1)
        accum = accum * jnp.transpose(factor, (2, 0, 1))[..., None]
        accum = contract_product(
            "bche,ebq->hbcq",
            weight_tensors.astype(jnp.bfloat16),
            value_portion.reshape(-1, KEY_HEADS, HEAD_SIZE),
        )
        return (new_peak, total, accum)

    live = jnp.logical_and(start <= last_query, start >= 0)
    peak, total, accum = lax.cond(live, attend_compute, lambda current: current, initial)
    attn_f32 = accum / jnp.transpose(total, (2, 0, 1))[..., None]
    log_total = peak + jnp.log(total)
    attn_low = attn_f32.reshape(rows, QW).astype(jnp.bfloat16)
    middle = hidden + jnp.dot(attn_low, w_output, preferred_element_type=jnp.float32)
    normed_two_f, factor_two = normalize(middle, gain_two)
    normed_two = normed_two_f.astype(jnp.bfloat16)
    gate = jnp.dot(normed_two, w_gate, preferred_element_type=jnp.float32)
    upward = jnp.dot(normed_two, w_upward, preferred_element_type=jnp.float32)
    sigma = jax.nn.sigmoid(gate)
    activated = gate * sigma
    inner = (activated * upward).astype(jnp.bfloat16)
    layer_out = (middle + jnp.dot(inner, w_down, preferred_element_type=jnp.float32)).astype(
        jnp.bfloat16
    )
    down_term = contract_product("tf,td->fd", inner, out_cotangent)
    inner_grad = contract_product("td,fd->tf", out_cotangent, w_down)
    gate_low = (inner_grad * upward * sigma * (1.0 + gate * (1.0 - sigma))).astype(jnp.bfloat16)
    upward_low = (inner_grad * activated).astype(jnp.bfloat16)
    gate_term = contract_product("td,tf->df", normed_two, gate_low)
    upward_term = contract_product("td,tf->df", normed_two, upward_low)
    normed_two_grad = contract_product("tf,df->td", gate_low, w_gate) + contract_product(
        "tf,df->td", upward_low, w_upward
    )
    middle_back, gain_two_term = normalize_back(middle, factor_two, gain_two, normed_two_grad)
    middle_grad = out_cotangent.astype(jnp.float32) + middle_back
    middle_low = middle_grad.astype(jnp.bfloat16)
    output_term = contract_product("tq,td->qd", attn_low, middle_low)
    attn_grad = contract_product("td,qd->tq", middle_low, w_output).astype(jnp.bfloat16)
    head_gradient = attn_grad.reshape(rows, KEY_HEADS, groups, HEAD_SIZE)
    delta = jnp.transpose(jnp.sum(head_gradient.astype(jnp.float32) * attn_f32, -1), (1, 2, 0))
    zero_query = jnp.zeros((rows, KEY_HEADS, groups, HEAD_SIZE), jnp.float32)
    empty_buffer = jnp.zeros((2, cycle * block, KW), jnp.float32)
    pieces = in_one_piece((key_block, value_block), "ctx", 0, 1)
    query_acc = zero_query
    buffer = empty_buffer
    grad_key_piece = pieces[0]
    grad_value_portion = pieces[1]

    def grad_compute(running_total):
        attention_logits, mask = scores_of(grad_key_piece)
        probabilities = jnp.where(mask, jnp.exp(attention_logits - log_total[..., None]), 0.0)
        key_head_rows = grad_key_piece.reshape(-1, KEY_HEADS, HEAD_SIZE)
        value_head_rows = grad_value_portion.reshape(-1, KEY_HEADS, HEAD_SIZE)
        value_increment = contract_product(
            "pjif,ipju->fpu", probabilities.astype(jnp.bfloat16), head_gradient
        )
        probability_gradient = contract_product("amxb,jmb->mxaj", head_gradient, value_head_rows)
        logit_gradient = (probabilities * (probability_gradient - delta[..., None])).astype(
            jnp.bfloat16
        )
        running_total = (
            contract_product("bche,ebq->hbcq", logit_gradient, key_head_rows) * score_scale
        )
        key_increment = (
            contract_product("pjif,ipju->fpu", logit_gradient, query_head_rows) * score_scale
        )
        return (
            running_total,
            jnp.stack([key_increment.reshape(-1, KW), value_increment.reshape(-1, KW)]),
        )

    def skip(running_total):
        return (running_total, jnp.zeros((2, grad_key_piece.shape[0], KW), jnp.float32))

    query_acc, added = lax.cond(jnp.int32(0) <= last_query, grad_compute, skip, query_acc)
    current = buffer
    buffer = added
    query_acc, all_grads = (query_acc, buffer)
    block_grads = lax.psum_scatter(all_grads, "ctx", scatter_dimension=1, tiled=True)
    key_sum, value_sum = sent_together(
        (block_grads[0].astype(jnp.bfloat16), block_grads[1].astype(jnp.bfloat16)), "fsdp", 0, 1
    )
    query_low = rotate_back(query_acc.reshape(rows, QW), cosine, sine).astype(jnp.bfloat16)
    key_low = rotate_back(key_sum, cosine, sine).astype(jnp.bfloat16)
    value_grad_low = value_sum.astype(jnp.bfloat16)
    query_term = contract_product("td,tq->dq", normed, query_low)
    key_term = contract_product("td,tq->dq", normed, key_low)
    value_term = contract_product("td,tq->dq", normed, value_grad_low)
    normed_grad = (
        contract_product("tq,dq->td", query_low, w_query)
        + contract_product("tq,dq->td", key_low, w_key)
        + contract_product("tq,dq->td", value_grad_low, w_value)
    )
    input_back, gain_one_term = normalize_back(hidden, factor_one, gain_one, normed_grad)
    input_grad = middle_grad + input_back
    gain_one_wide = jnp.broadcast_to(gain_one_term[:, None], (gain_one_term.shape[0], pair))
    gain_two_wide = jnp.broadcast_to(gain_two_term[:, None], (gain_two_term.shape[0], pair))
    summed = (
        summed_on_arrival(query_term.astype(jnp.bfloat16), "fsdp", 1),
        *sent_together(
            (key_term.astype(jnp.bfloat16), value_term.astype(jnp.bfloat16)), "fsdp", 1, 0
        ),
        summed_on_arrival(output_term.astype(jnp.bfloat16), "fsdp", 1),
        *sent_together(
            (gate_term.astype(jnp.bfloat16), upward_term.astype(jnp.bfloat16)), "fsdp", 1, 0
        ),
        summed_on_arrival(down_term.astype(jnp.bfloat16), "fsdp", 1),
        *sent_together(
            (gain_one_wide.astype(jnp.bfloat16), gain_two_wide.astype(jnp.bfloat16)), "fsdp", 1, 0
        ),
    )
    owned = sum_packed(
        (
            summed[7][:, 0],
            summed[8][:, 0],
            summed[0],
            summed[1],
            summed[2],
            summed[3],
            summed[4],
            summed[5],
            summed[6],
        ),
        "ctx",
        (0, 0, 0, 0, 0, 0, 0, 0, 0),
    )
    return (
        layer_out,
        input_grad,
        owned[0],
        owned[2],
        owned[3],
        owned[4],
        owned[5],
        owned[1],
        owned[6],
        owned[7],
        owned[8],
    )


def solution(mesh):
    return jax.shard_map(
        local,
        mesh=mesh,
        in_specs=(
            P(("ctx", "fsdp"), None),
            P("ctx"),
            P("ctx", "fsdp"),
            P("ctx", "fsdp"),
            P("ctx", "fsdp"),
            P("ctx", "fsdp"),
            P("ctx"),
            P("ctx", "fsdp"),
            P("ctx", "fsdp"),
            P("ctx", "fsdp"),
            P(("ctx", "fsdp"), None),
        ),
        out_specs=(
            P(("ctx", "fsdp"), None),
            P(("ctx", "fsdp"), None),
            P("ctx"),
            P("ctx", "fsdp"),
            P("ctx", "fsdp"),
            P("ctx", "fsdp"),
            P("ctx", "fsdp"),
            P("ctx"),
            P("ctx", "fsdp"),
            P("ctx", "fsdp"),
            P("ctx", "fsdp"),
        ),
        check_vma=False,
    )
```

profile of v0, /device:TPU:0, one launch (start us, length us, event | category | flops | bytes accessed | tf_op | source)
XLA Modules:
  0.0 1946.0 jit_solution(16970652136435008527)
XLA Ops:
  10.5 86.9 %all-gather.24.cloned.1.call-done = bf16[64,15,3841]{2,1,0:T(8,128)(2,1)} async-done(((bf16[1,15,3841]{2,1,0:T(8,128)(2,1)}), bf16[64,15,3841]{2,1,0:T(8,128)(2,1)}) %all-gather.24.cloned.1.call-update) | async-done | bytes 7374736 | tf_op jit(solution)/shard_map/all_gather | solution.py:21
  97.3 10.2 reshape.279
  111.1 55.7 %all-gather.20.cloned.1.call-done = bf16[2560,480]{1,0:T(8,128)(2,1)} async-done(((bf16[40,480]{1,0:T(8,128)(2,1)}), bf16[2560,480]{1,0:T(8,128)(2,1)}) %all-gather.20.cloned.1.call-update) | async-done | bytes 2457616 | tf_op jit(solution)/shard_map/all_gather | solution.py:153
  166.8 4.5 copy.70
  177.2 166.6 %all-reduce.1 = bf16[960]{0:T(1024)(128)(2,1)S(1)} all-reduce(bf16[960]{0:T(1024)(128)(2,1)S(1)} %dynamic-update-slice), channel_id=1, replica_groups=mesh['ctx'=64,'fsdp'=2] {'ctx'}, use_global_device_ids=true, to_apply=%add.1 | all-reduce | flops 960 | bytes 3840
  348.0 6.1 all_gather.34
  355.7 5.3 fusion.68
  372.2 132.2 %all-gather.12.cloned.1.call-done = bf16[16384,640]{0,1:T(8,128)(2,1)} async-done(((bf16[256,640]{0,1:T(8,128)(2,1)}), bf16[16384,640]{0,1:T(8,128)(2,1)}) %all-gather.12.cloned.1.call-update) | async-done | bytes 20971536 | tf_op jit(solution)/shard_map/all_gather | solution.py:32
  504.4 16.3 fusion.66
  520.7 140.3 %conditional.2 = (f32[5,3,128]{2,1,0:T(4,128)}, f32[5,3,128]{2,1,0:T(4,128)}, f32[128,5,3,64]{0,3,2,1:T(8,128)}, f32[5,3,128]{2,1,0:T(4,128)S(1)}) conditional(s32[]{:T(128)} %convert_element_type.158, () %tuple.32, (s32[128]{0:T(128)S(1)}, bf16[16384,320]{0,1:T(8,128)(2,1)}, bf16[128,5,3,64]{0,3,2,1:T(8,128)(2,1)S(1)}, ...), branch_computations={%region_1.0_spmd, %region_2.5_spmd} | conditional | flops 8401188864 | bytes 407646752 | solution.py:214
  522.2 52.3 %fusion = (f32[5,3,128]{2,1,0:T(4,128)S(1)}, f32[5,16384,128,3]{2,1,3,0:T(8,128)}) fusion(pred[128,16384]{0,1:T(8,128)(4,1)S(1)} %iota_compare_fusion, bf16[16384,5,64,1]{0,2,3,1:T(8,128)(2,1)} %bitcast.2, bf16[128,5,3,64]{0,3,2,1:T(8,128)(2,1)S(1)} %get-tuple-element.45), kind=kOutput, calls=%fused_computation.2 | convolution fusion | flops 4120901632 | bytes 138665472 | tf_op jit(solution)/shard_map/cond/branch_1_fun/amxb,jmb->mxaj/dot_general | solution.py:71
  575.0 39.2 %fusion.4 = f32[5,3,128]{2,1,0:T(4,128)} fusion(f32[5,16384,128,3]{2,1,3,0:T(8,128)} %get-tuple-element.85, f32[5,3,128]{2,1,0:T(4,128)} %broadcast_maximum_fusion, pred[128,16384]{0,1:T(8,128)(4,1)S(1)} %iota_compare_fusion), kind=kLoop, calls=%fused_computation.6 | loop fusion | flops 125827200 | bytes 127941632 | tf_op jit(solution)/shard_map/cond/branch_1_fun/reduce_sum | solution.py:204
  614.2 46.1 %fusion.8 = f32[128,5,3,64]{0,3,2,1:T(8,128)} fusion(bf16[16384,5,64,1]{0,2,3,1:T(8,128)(2,1)} %bitcast.160, f32[5,16384,128,3]{2,1,3,0:T(8,128)} %get-tuple-element.85, f32[5,3,128]{2,1,0:T(4,128)} %broadcast_maximum_fusion, pred[128,16384]{0,1:T(8,128)(4,1)S(1)} %iota_compare_fusion), kind=kOutput, calls=%fused_computation.10 | convolution fusion | flops 4152360960 | bytes 138911232 | tf_op jit(solution)/shard_map/cond/branch_1_fun/bche,ebq->hbcq/dot_general | solution.py:71
  668.4 4.8 multiply_convert_fusion.1
  679.8 266.1 %conditional.3 = (f32[2,16384,320]{1,2,0:T(8,128)}, f32[128,15,32]{0,2,1:T(8,128)}, f32[128,15,32]{0,2,1:T(8,128)}) conditional(s32[]{:T(128)} %convert_element_type.158, () %tuple.34, (s32[128]{0:T(128)S(1)}, bf16[16384,320]{0,1:T(8,128)(2,1)}, bf16[128,5,3,64]{0,3,2,1:T(8,128)(2,1)S(1)}, f32[5,3,128]{2,1,0:T(4,128)}, f32[5,3,128]{2,1,0:T(4,128)S(1)}, ...), branch_computations={%region_8.9_spmd, %region_9.10_spmd} | conditional | flops 20465182720 | bytes 734279232 | solution.py:279
  679.8 46.0 %fusion.78 = f32[5,16384,128,3]{2,1,3,0:T(8,128)} fusion(bf16[16384,5,64,1]{0,2,3,1:T(8,128)(2,1)} %bitcast.10, bf16[128,5,3,64]{0,3,2,1:T(8,128)(2,1)S(1)} %get-tuple-element.49), kind=kOutput, calls=%fused_computation.145 | convolution fusion | flops 4026531840 | bytes 136560640 | tf_op jit(solution)/shard_map/cond/branch_1_fun/amxb,jmb->mxaj/dot_general | solution.py:71
  727.9 51.2 %fusion.18 = f32[5,16384,64,1]{1,2,3,0:T(8,128)} fusion(bf16[128,5,3,64]{0,3,2,1:T(8,128)(2,1)S(1)} %get-tuple-element.53, f32[5,16384,128,3]{2,1,3,0:T(8,128)} %fusion.78, f32[5,3,128]{2,1,0:T(4,128)S(1)} %add.68, pred[128,16384]{0,1:T(8,128)(4,1)S(1)} %iota_compare_fusion.1), kind=kOutput, calls=%fused_computation.21 | convolution fusion | flops 4152360960 | bytes 149151232 | tf_op jit(solution)/shard_map/cond/branch_1_fun/pjif,ipju->fpu/dot_general | solution.py:71
  779.1 78.1 %fusion.14 = bf16[5,3,128,16384]{2,3,1,0:T(8,128)(2,1)} fusion(f32[5,16384,128,3]{2,1,3,0:T(8,128)} %fusion.78, f32[5,3,128]{2,1,0:T(4,128)S(1)} %get-tuple-element.54, f32[5,3,128]{2,1,0:T(4,128)S(1)} %add.68, pred[128,16384]{0,1:T(8,128)(4,1)S(1)} %iota_compare_fusion.1, bf16[16384,5,64,1]{0,2,3,1:T(8,128)(2,1)} %bitcast.161, ...), kind=kOutput, calls=%fused_computation.16 | convolution fusion | flops 4215275520 | bytes 201587712 | tf_op jit(solution)/shard_map/cond/branch_1_fun/amxb,jmb->mxaj/dot_general | solution.py:71
  857.2 34.0 %fusion.21 = f32[5,16384,64]{1,2,0:T(8,128)} fusion(bf16[5,3,128,16384]{2,3,1,0:T(8,128)(2,1)} %fusion.14, bf16[128,5,3,64]{0,3,2,1:T(8,128)(2,1)S(1)} %copy-done.18), kind=kOutput, calls=%fused_computation.25 | convolution fusion | flops 4031774720 | bytes 84131840 | tf_op jit(solution)/shard_map/cond/branch_1_fun/pjif,ipju->fpu/dot_general | solution.py:71
  891.2 28.0 %pad_maximum_fusion = f32[2,16384,320]{1,2,0:T(8,128)} fusion(f32[1,16384,320]{1,2,0:T(8,128)} %bitcast.159, f32[1,16384,320]{1,2,0:T(8,128)} %bitcast.155), kind=kLoop, calls=%fused_computation.23 | loop fusion | flops 10485760 | bytes 83886080 | tf_op jit(solution)/shard_map/cond/branch_1_fun/stack | solution.py:273
  919.3 25.8 %convolution_multiply_fusion = f32[5,3,128,64]{2,3,1,0:T(8,128)S(1)} fusion(bf16[16384,5,64,1]{0,2,3,1:T(8,128)(2,1)} %bitcast.10, bf16[5,3,128,16384]{2,3,1,0:T(8,128)(2,1)} %fusion.14), kind=kOutput, calls=%fused_computation.27 | convolution fusion | flops 4026654720 | bytes 73891840 | tf_op jit(solution)/shard_map/cond/branch_1_fun/bche,ebq->hbcq/dot_general | solution.py:71
  955.7 43.1 %all-to-all-done.2 = bf16[2,960,480]{1,2,0:T(8,128)(2,1)S(1)} async-done(((bf16[2,960,480]{1,2,0:T(8,128)(2,1)}), bf16[2,960,480]{1,2,0:T(8,128)(2,1)S(1)}, u32[]{:S(2)}, u32[]{:S(2)}) %all-to-all-start.2) | async-done | bytes 1843232 | tf_op jit(solution)/shard_map/all_to_all | solution.py:43
  998.7 4.7 all-to-all-start.4
  1003.5 4.8 convolution_convert_fusion
  1008.3 45.0 %all-to-all-done.4 = bf16[2,960,480]{1,2,0:T(8,128)(2,1)} async-done(((bf16[2,960,480]{1,2,0:T(8,128)(2,1)}), bf16[2,960,480]{1,2,0:T(8,128)(2,1)}, u32[]{:S(2)}, u32[]{:S(2)}) %all-to-all-start.4) | async-done | bytes 1843232 | tf_op jit(solution)/shard_map/all_to_all | solution.py:43
  1053.3 5.9 all-to-all-start.6
  1067.7 8.3 copy.92
  1076.0 108.5 %all-to-all-done.6 = bf16[2,2560,480]{1,2,0:T(8,128)(2,1)} async-done(((bf16[2,2560,480]{1,2,0:T(8,128)(2,1)}), bf16[2,2560,480]{1,2,0:T(8,128)(2,1)}, u32[]{:S(2)}, u32[]{:S(2)}) %all-to-all-start.6) | async-done | bytes 4915232 | tf_op jit(solution)/shard_map/all_to_all | solution.py:43
  1184.5 7.4 all-to-all-start.5
  1205.0 6.0 convert_reduce_fusion.1
  1211.0 5.8 copy.78
  1216.8 6.7 reshape_reshape.34
  1223.5 130.8 %reduce-scatter.3.cloned.1.call-done = f32[2,256,320]{1,2,0:T(8,128)} async-done(((f32[2,16384,320]{1,2,0:T(8,128)}), f32[2,256,320]{1,2,0:T(8,128)}) %reduce-scatter.3.cloned.1.call-update) | async-done | bytes 655376 | tf_op jit(solution)/shard_map/reduce_scatter | solution.py:283
  1356.8 31.2 %all-to-all-done.5 = bf16[2,1920,1280]{2,1,0:T(8,128)(2,1)} async-done(((bf16[2,1920,1280]{2,1,0:T(8,128)(2,1)}), bf16[2,1920,1280]{2,1,0:T(8,128)(2,1)}, u32[]{:S(2)}, u32[]{:S(2)}) %all-to-all-start.5) | async-done | bytes 9830432 | tf_op jit(solution)/shard_map/all_to_all | solution.py:43
  1391.4 10.0 convert_reduce_fusion
  1418.9 4.5 all-to-all-start.3
  1423.4 8.3 fusion.67
  1431.8 5.7 reshape_reshape.32
  1437.5 5.7 reshape_reshape.33
  1446.8 8.1 dynamic-update-slice.3
  1472.8 7.2 dynamic-update-slice.6
  1480.0 17.6 dynamic-update-slice.7
  1497.5 17.5 dynamic-update-slice.8
  1515.1 17.0 dynamic-update-slice.9
  1532.1 15.0 pad.4
  1547.0 16.1 reshape.265
  1564.4 4.5 fusion.37
  1569.9 359.9 %reduce-scatter.5.cloned.1.call-done = f32[608,128]{1,0:T(8,128)} async-done(((f32[38912,128]{1,0:T(8,128)}), f32[608,128]{1,0:T(8,128)}) %reduce-scatter.5.cloned.1.call-update) | async-done | bytes 311312 | tf_op jit(solution)/shard_map/reduce_scatter | solution.py:62
  (229 shorter events, 135.1 us)
Async XLA Ops:
  7.2 90.1 %all-gather.24.cloned.1.call-start = ((), (), s32[]{:S(2)}) async-start(), calls=%async_computation.18 | async-start | bytes 8253440 | tf_op jit(solution)/shard_map/all_gather | solution.py:21
  9.7 157.1 %all-gather.20.cloned.1.call-start = ((), (), s32[]{:S(2)}) async-start(), calls=%async_computation.14 | async-start | bytes 2662400 | tf_op jit(solution)/shard_map/all_gather | solution.py:153
  10.4 334.3 %all-gather.10.cloned.1.call-start = ((), (), s32[]{:S(2)}) async-start(), calls=%async_computation.9 | async-start | bytes 1843200 | tf_op jit(solution)/shard_map/all_gather | solution.py:32
  107.5 63.8 %copy-start.43 = (u32[128]{0:T(128)S(1)}, u32[128]{0:T(128)}, u32[]{:S(2)}) copy-start(u32[128]{0:T(128)} %constant.79) | copy-start | bytes 1540
  107.5 65.1 %copy-start.42 = (bf16[15]{0:T(256)(128)(2,1)S(1)}, bf16[15]{0:T(256)(128)(2,1)}, u32[]{:S(2)}) copy-start(bf16[15]{0:T(256)(128)(2,1)} %param.16) | copy-start | bytes 94
  109.5 234.3 %copy-start = (bf16[128,960]{0,1:T(8,128)(2,1)S(1)}, bf16[128,960]{0,1:T(8,128)(2,1)}, u32[]{:S(2)}) copy-start(bf16[128,960]{0,1:T(8,128)(2,1)} %param.15) | copy-start | bytes 737284
  111.0 252.7 %all-gather.22.cloned.1.call-start = ((), (), s32[]{:S(2)}) async-start(), calls=%async_computation.15 | async-start | bytes 7372800 | tf_op jit(solution)/shard_map/all_gather | solution.py:162
  171.3 198.5 %all-gather.14.cloned.1.call-start = ((), (), s32[]{:S(2)}) async-start(), calls=%async_computation.11 | async-start | bytes 2949120 | tf_op jit(solution)/shard_map/all_gather | solution.py:158
  177.2 327.2 %all-gather.12.cloned.1.call-start = ((), (), s32[]{:S(2)}) async-start(), calls=%async_computation.10 | async-start | bytes 21299200 | tf_op jit(solution)/shard_map/all_gather | solution.py:32
  343.8 25.9 %copy-start.31 = (f32[960]{0:T(1024)}, f32[960]{0:T(1024)S(1)}, u32[]{:S(2)}) copy-start(f32[960]{0:T(1024)S(1)} %convert_element_type.159) | copy-start | bytes 11524
  344.5 25.2 %copy-start.36 = (f32[128]{0:T(128)}, f32[128]{0:T(128)S(1)}, u32[]{:S(2)}) copy-start(f32[128]{0:T(128)S(1)} %get-tuple-element.127) | copy-start | bytes 1540
  344.7 27.4 %copy-start.27 = (f32[128,32]{0,1:T(8,128)}, f32[128,32]{0,1:T(8,128)S(1)}, u32[]{:S(2)}) copy-start(f32[128,32]{0,1:T(8,128)S(1)} %get-tuple-element.124) | copy-start | bytes 49156
  344.7 27.4 %copy-start.29 = (f32[128,32]{0,1:T(8,128)}, f32[128,32]{0,1:T(8,128)S(1)}, u32[]{:S(2)}) copy-start(f32[128,32]{0,1:T(8,128)S(1)} %get-tuple-element.125) | copy-start | bytes 49156
  354.1 308.2 %all-gather.16.cloned.1.call-start = ((), (), s32[]{:S(2)}) async-start(), calls=%async_computation.12 | async-start | bytes 2949120 | tf_op jit(solution)/shard_map/all_gather | solution.py:160
  355.7 309.4 %all-gather.18.cloned.1.call-start = ((), (), s32[]{:S(2)}) async-start(), calls=%async_computation.13 | async-start | bytes 14745600 | tf_op jit(solution)/shard_map/all_gather | solution.py:32
  363.6 990.7 %reduce-scatter.3.cloned.1.call-start = ((), (), s32[]{:S(2)}) async-start(), calls=%async_computation.16 | async-start | bytes 42598400 | tf_op jit(solution)/shard_map/reduce_scatter | solution.py:283
  363.6 157.1 %copy-start.38 = (s32[128]{0:T(128)}, s32[128]{0:T(128)S(1)}, u32[]{:S(2)}) copy-start(s32[128]{0:T(128)S(1)} %iota_add_fusion) | copy-start | bytes 1540
  520.7 141.6 %copy-start.1 = (bf16[128,960]{0,1:T(8,128)(2,1)S(1)}, bf16[128,960]{0,1:T(8,128)(2,1)}, u32[]{:S(2)}) copy-start(bf16[128,960]{0,1:T(8,128)(2,1)} %param.15) | copy-start | bytes 737284
  520.7 143.9 %copy-start.35 = (f32[960]{0:T(1024)S(1)}, f32[960]{0:T(1024)}, u32[]{:S(2)}) copy-start(f32[960]{0:T(1024)} %convert_reduce_fusion.6) | copy-start | bytes 11524
  661.1 7.3 copy-start.23
  662.3 10.9 copy-start.20
  664.6 12.8 copy-start.4
  664.9 8.3 copy-start.10
  668.3 5.5 copy-start.16
  673.2 4.4 copy-start.24
  673.2 4.4 copy-start.26
  675.3 4.5 copy-start.34
  675.3 4.5 copy-start.39
  679.8 46.1 %copy-start.17 = (bf16[128,5,3,64]{0,3,2,1:T(8,128)(2,1)}, bf16[128,5,3,64]{0,3,2,1:T(8,128)(2,1)S(1)}, u32[]{:S(2)}) copy-start(bf16[128,5,3,64]{0,3,2,1:T(8,128)(2,1)S(1)} %get-tuple-element.49) | copy-start | bytes 737284 | tf_op jit(solution)/shard_map/cond
  779.1 78.1 %copy-start.18 = (bf16[128,5,3,64]{0,3,2,1:T(8,128)(2,1)S(1)}, bf16[128,5,3,64]{0,3,2,1:T(8,128)(2,1)}, u32[]{:S(2)}) copy-start(bf16[128,5,3,64]{0,3,2,1:T(8,128)(2,1)} %copy-done.17) | copy-start | bytes 737284 | tf_op jit(solution)/shard_map/cond
  945.9 7.8 copy-start.8
  945.9 7.8 copy-start.21
  946.0 57.6 %copy-start.14 = (bf16[128,960]{0,1:T(8,128)(2,1)S(1)}, bf16[128,960]{0,1:T(8,128)(2,1)}, u32[]{:S(2)}) copy-start(bf16[128,960]{0,1:T(8,128)(2,1)} %param.25) | copy-start | bytes 737284
  947.8 55.7 %copy-start.19 = (bf16[128,15,64]{0,2,1:T(8,128)(2,1)}, bf16[128,15,64]{0,2,1:T(8,128)(2,1)S(1)}, u32[]{:S(2)}) copy-start(bf16[128,15,64]{0,2,1:T(8,128)(2,1)S(1)} %pad_maximum_fusion.7) | copy-start | bytes 737284
  949.9 48.8 %all-to-all-start.2 = ((bf16[2,960,480]{1,2,0:T(8,128)(2,1)}), bf16[2,960,480]{1,2,0:T(8,128)(2,1)S(1)}, u32[]{:S(2)}, u32[]{:S(2)}) async-start(bf16[2,960,480]{1,2,0:T(8,128)(2,1)} %bitcast.163), calls=%async_computation.3 | async-start | bytes 3932160 | tf_op jit(solution)/shard_map/all_to_all | solution.py:43
  998.7 54.5 %all-to-all-start.4 = ((bf16[2,960,480]{1,2,0:T(8,128)(2,1)}), bf16[2,960,480]{1,2,0:T(8,128)(2,1)}, u32[]{:S(2)}, u32[]{:S(2)}) async-start(bf16[2,960,480]{1,2,0:T(8,128)(2,1)} %bitcast.162), calls=%async_computation.5 | async-start | bytes 3932160 | tf_op jit(solution)/shard_map/all_to_all | solution.py:43
  1003.5 55.6 %copy-start.11 = (bf16[128,960]{0,1:T(8,128)(2,1)S(1)}, bf16[128,960]{0,1:T(8,128)(2,1)}, u32[]{:S(2)}) copy-start(bf16[128,960]{0,1:T(8,128)(2,1)} %copy-done.10) | copy-start | bytes 737284
  1053.3 131.2 %all-to-all-start.6 = ((bf16[2,2560,480]{1,2,0:T(8,128)(2,1)}), bf16[2,2560,480]{1,2,0:T(8,128)(2,1)}, u32[]{:S(2)}, u32[]{:S(2)}) async-start(bf16[2,2560,480]{1,2,0:T(8,128)(2,1)} %bitcast.158), calls=%async_computation.7 | async-start | bytes 9830400 | tf_op jit(solution)/shard_map/all_to_all | solution.py:43
  1184.5 203.5 %all-to-all-start.5 = ((bf16[2,1920,1280]{2,1,0:T(8,128)(2,1)}), bf16[2,1920,1280]{2,1,0:T(8,128)(2,1)}, u32[]{:S(2)}, u32[]{:S(2)}) async-start(bf16[2,1920,1280]{2,1,0:T(8,128)(2,1)} %bitcast.156), calls=%async_computation.6 | async-start | bytes 19660800 | tf_op jit(solution)/shard_map/all_to_all | solution.py:43
  1388.0 13.5 all-to-all-start
  1391.4 15.4 copy-start.3
  1401.4 8.1 copy-start.40
  1411.5 7.3 all-to-all-start.1
  1418.9 36.0 %all-to-all-start.3 = ((bf16[2,1920,160]{1,2,0:T(8,128)(2,1)}), bf16[2,1920,160]{1,2,0:T(8,128)(2,1)}, u32[]{:S(2)}, u32[]{:S(2)}) async-start(bf16[2,1920,160]{1,2,0:T(8,128)(2,1)} %bitcast.48), calls=%async_computation.4 | async-start | bytes 2457600 | tf_op jit(solution)/shard_map/all_to_all | solution.py:43
  1423.4 506.4 %reduce-scatter.5.cloned.1.call-start = ((), (), s32[]{:S(2)}) async-start(), calls=%async_computation.17 | async-start | bytes 20234240 | tf_op jit(solution)/shard_map/reduce_scatter | solution.py:62
  1446.8 26.0 %copy-start.9 = (f32[64,7200]{1,0:T(8,128)S(1)}, f32[64,7200]{1,0:T(8,128)}, u32[]{:S(2)}) copy-start(f32[64,7200]{1,0:T(8,128)} %reshape_reshape.31) | copy-start | bytes 5529604
  1563.2 5.8 copy-start.22
  1563.2 5.8 copy-start.41
  (13 other events, 25.1 us)
Sparse Core Ops, SparseCore 0:
  11.7 85.5 all-gather.23
  100.4 66.2 all-gather.19
  168.4 22.6 all-gather.9
  192.7 68.8 all-gather.21
  263.0 34.9 all-gather.13
  354.2 150.1 all-gather.11
  506.1 31.3 all-gather.15
  539.2 125.8 all-gather.17
  946.1 408.1 reduce-scatter.2
  1563.3 366.4 reduce-scatter.4
where the time goes:
time: 1960 us; the launch traced here: 1950 us
  waiting for transfers between devices  996 us (51%)
  matrix products  384 us (20%)
  local copies, waits for them, and re-layouts  232 us (12%)
  blocking collectives  173 us (9%)
  other arithmetic  113 us (6%)
  starting transfers between devices  33.7 us (2%)
    dot_general x21, matrix products, contract_product(): return jnp.einsum(form, left, right, preferred_element_type=jnp.float32)  363 us
    reduce_scatter x1, waiting for transfers between devices, sum_packed(): lax.psum_scatter(lines, axis, tiled=True).reshape(-1)  360 us
    all_to_all x7, waiting for transfers between devices, summed_on_arrival(): parts = lax.all_to_all(in_blocks(x, dim, count), axis, 0, 0, tiled=True)  229 us
    unnamed x1, blocking collectives  167 us
    all_gather x3, waiting for transfers between devices, in_one_piece(): out = lax.all_gather(both, axis, axis=dim, tiled=True)  132 us
    reduce_scatter x1, waiting for transfers between devices, local(): lax.psum_scatter(all_grads, 'ctx', scatter_dimension=1, tiled=True)  131 us
    all_gather x1, waiting for transfers between devices, side_by_side(): lax.all_gather(both, axis, axis=dim, tiled=True)  86.9 us
    unnamed x99, local copies, waits for them, and re-layouts  76.2 us
  transfers between devices with their start and end apart: 17, of which 11 were waited for; matrix products, arithmetic and copies ran while one was open for 16% of the time, Pallas kernels for 0%

commit v1 on v0

v1 whole, which is shorter than its diff:
```python
import functools

import jax
import jax.numpy as jnp
from jax import lax
from jax.experimental import pallas as pl
from jax.experimental.pallas import tpu as pltpu
from jax.sharding import PartitionSpec as P

MESH = pl.DeviceIdType.MESH
ORDERS = (("x", "y", "z"), ("y", "z", "x"), ("z", "x", "y"))
ALL = slice(None)


def whereabouts():
    ctx = lax.axis_index("ctx")
    low = lax.axis_index("fsdp")
    return {
        "x": lax.rem(lax.div(ctx, 8), 4),
        "y": lax.rem(lax.div(ctx, 2), 4),
        "z": lax.div(ctx, 32) * 2 + low,
        "c": lax.rem(ctx, 2),
    }


def device_at(at):
    ctx = ((lax.div(at["z"], 2) * 4 + at["x"]) * 4 + at["y"]) * 2 + at["c"]
    return (ctx, lax.rem(at["z"], 2))


def moved(at, axis, by):
    size = 2 if axis == "c" else 4
    return {**at, axis: lax.rem(at[axis] + by + size, size)}


def greet(me):
    barrier = pltpu.get_barrier_semaphore()
    others = [moved(me, a, s) for a in "xyz" for s in (1, -1)] + [moved(me, "c", 1)]
    for other in others:
        pl.semaphore_signal(barrier, inc=1, device_id=device_at(other), device_id_type=MESH)
    pl.semaphore_wait(barrier, len(others))


def place(dims, at):
    index = []
    for d in dims:
        if d in ("zh", "zl"):
            z = at["z"]
            index.append(ALL if z is ALL else (lax.div(z, 2) if d == "zh" else lax.rem(z, 2)))
        elif d == "l":
            index.append(at.get("l", ALL))
        else:
            index.append(at[d])
    return index


def view(ref, dims, at, cols, half=None):
    start, width = cols
    if half is not None:
        if "l" in dims:
            at = {**at, "l": half}
        else:
            start, width = start + half * (width // 2), width // 2
    return ref.at[tuple(place(dims, at)) + (ALL, pl.ds(start, width))]


def gather_kernel(dims, parts, piece_ref, out_ref, send, recv, sib_send, sib_recv, own_sem):
    me = whereabouts()
    greet(me)
    sibling = device_at(moved(me, "c", 1))
    lead = (ALL,) if "l" in dims else ()

    def copy(src, dst, ssem, rsem, to):
        c = pltpu.make_async_remote_copy(
            src_ref=src, dst_ref=dst, send_sem=ssem, recv_sem=rsem, device_id=to, device_id_type=MESH
        )
        c.start()
        return c

    pending = []
    mine = out_ref.at[tuple(place(dims, me)) + (ALL, ALL)]
    own = pltpu.make_async_copy(piece_ref, mine, own_sem)
    own.start()
    own.wait()
    for phase in range(3):
        stage = {}
        for i, cols in enumerate(parts):
            order = ORDERS[i]
            axis = order[phase]
            base = dict(me)
            for done in order[:phase]:
                base[done] = ALL
            right, left = moved(me, axis, 1), moved(me, axis, -1)

            def blk(by, half=None, base=base, axis=axis, cols=cols):
                at = {**base, axis: lax.rem(me[axis] + by + 4, 4)}
                return view(out_ref, dims, at, cols, half)

            s, r = send.at[i, phase], recv.at[i, phase]
            to_right = copy(blk(0), blk(0), s.at[0], r.at[0], device_at(right))
            to_left = copy(blk(0), blk(0), s.at[1], r.at[1], device_at(left))
            sibs = []
            if phase == 2:
                sibs.append(copy(blk(0), blk(0), sib_send.at[i, 0], sib_recv.at[i, 0], sibling))
            stage[i] = (blk, s, r, to_right, to_left, sibs, right, left)
        for i in range(len(parts)):
            blk, s, r, to_right, to_left, sibs, right, left = stage[i]
            to_right.wait_recv()
            on_right = copy(blk(-1, 0), blk(-1, 0), s.at[2], r.at[2], device_at(right))
            if phase == 2:
                sibs.append(copy(blk(-1), blk(-1), sib_send.at[i, 1], sib_recv.at[i, 1], sibling))
            to_left.wait_recv()
            on_left = copy(blk(1, 1), blk(1, 1), s.at[3], r.at[3], device_at(left))
            if phase == 2:
                sibs.append(copy(blk(1), blk(1), sib_send.at[i, 2], sib_recv.at[i, 2], sibling))
            pending += [to_right, to_left, on_right, on_left]
            stage[i] = (blk, sibs, on_right, on_left)
        for i in range(len(parts)):
            blk, sibs, on_right, on_left = stage[i]
            on_right.wait_recv()
            on_left.wait_recv()
            if phase == 2:
                sibs.append(copy(blk(2), blk(2), sib_send.at[i, 3], sib_recv.at[i, 3], sibling))
                pending += sibs
        if phase == 2:
            for i in range(len(parts)):
                for c in stage[i][1]:
                    c.wait_recv()
    for c in pending:
        c.wait_send()


SIZE = {"zl": 2, "zh": 2, "x": 4, "y": 4, "c": 2, "l": 2}


def gather(piece, dims, parts, name, collective_id):
    shape = tuple(SIZE[d] for d in dims) + piece.shape[-2:]
    n = len(parts)
    return pl.pallas_call(
        functools.partial(gather_kernel, dims, parts),
        out_shape=jax.ShapeDtypeStruct(shape, piece.dtype),
        in_specs=[pl.BlockSpec(memory_space=pl.ANY)],
        out_specs=pl.BlockSpec(memory_space=pl.ANY),
        scratch_shapes=[
            pltpu.SemaphoreType.DMA((n, 3, 4)),
            pltpu.SemaphoreType.DMA((n, 3, 4)),
            pltpu.SemaphoreType.DMA((n, 4)),
            pltpu.SemaphoreType.DMA((n, 4)),
            pltpu.SemaphoreType.DMA,
        ],
        compiler_params=pltpu.CompilerParams(collective_id=collective_id, has_side_effects=True),
        name=name,
    )(piece)


def scatter_kernel(dims, parts, n_in, *refs):
    ins, out_ref, refs = refs[:n_in], refs[n_in], refs[n_in + 1 :]
    n = len(parts)
    work, sib = refs[:n], refs[n : 2 * n]
    bufs = refs[2 * n : 2 * n + 12 * n]
    load_sem, sib_send, sib_recv, send, recv = refs[14 * n :]
    wdims = tuple(d for d in dims if d != "c")
    me = whereabouts()
    other = moved(me, "c", 1)
    sibling = device_at(other)
    widths = [w.shape[-1] for w in work]
    starts = [sum(widths[:i]) for i in range(n)]

    def remote(src, dst, ssem, rsem, to):
        c = pltpu.make_async_remote_copy(
            src_ref=src, dst_ref=dst, send_sem=ssem, recv_sem=rsem, device_id=to, device_id_type=MESH
        )
        c.start()
        return c

    loads, pairs = {}, {}
    TURN = (2, 1, -1, 0)

    def own_loads(step):
        for i, sources in enumerate(parts):
            axis = ORDERS[i][0]
            at = {"x": ALL, "y": ALL, "z": ALL, "c": me["c"], axis: lax.rem(me[axis] + TURN[step] + 4, 4)}
            loads[i, step] = []
            for j, (k, (c0, width), d0) in enumerate(sources):
                c = pltpu.make_async_copy(
                    view(ins[k], dims, at, (c0, width)),
                    view(work[i], wdims, at, (d0, width)),
                    load_sem.at[i, step, j],
                )
                c.start()
                loads[i, step].append(c)

    def sib_sends(step):
        for i, sources in enumerate(parts):
            axis = ORDERS[i][0]
            at = {"x": ALL, "y": ALL, "z": ALL, "c": other["c"], axis: lax.rem(me[axis] + TURN[step] + 4, 4)}
            pairs[i, step] = []
            for j, (k, (c0, width), d0) in enumerate(sources):
                pairs[i, step].append(
                    remote(
                        view(ins[k], dims, at, (c0, width)),
                        view(sib[i], wdims, at, (d0, width)),
                        sib_send.at[i, step, j],
                        sib_recv.at[i, step, j],
                        sibling,
                    )
                )

    own_loads(0)
    greet(me)
    for step in range(4):
        sib_sends(step)
        if step:
            own_loads(step)
    pending = []

    def each_block(at, body):
        free = [d for d in wdims if (at["z"] if d in ("zh", "zl") else at.get(d, ALL)) is ALL]
        total = 1
        for d in free:
            total *= SIZE[d]

        def one(t, _):
            vals, rest = {}, t
            for d in reversed(free):
                vals[d] = lax.rem(rest, SIZE[d])
                rest = lax.div(rest, SIZE[d])
            full = []
            for d, fixed in zip(wdims, place(wdims, at)):
                full.append(vals[d] if d in vals else fixed)
            body(tuple(full), tuple(vals[d] for d in free))
            return 0

        if total == 1:
            one(jnp.int32(0), 0)
        else:
            lax.fori_loop(0, total, one, 0)

    f32 = jnp.float32

    def add(i, at, others, half=None, out=None):
        w = widths[i]
        lo, size = 0, w
        if half is not None:
            if "l" in wdims:
                at = {**at, "l": half}
            else:
                lo, size = half * (w // 2), w // 2

        def body(full, short):
            cut = (ALL, pl.ds(lo, size))
            total = work[i][full + cut].astype(f32)
            for ref, same in others:
                if same:
                    total = total + ref[full + cut].astype(f32)
                else:
                    total = total + ref[short + (ALL, ALL)].astype(f32)
            if out is None:
                work[i][full + cut] = total.astype(work[i].dtype)
            else:
                lead = (full[0],) if "l" in wdims else ()
                out[lead + (ALL, pl.ds(starts[i], w))] = total

        each_block(at, body)

    for phase in range(3):
        stage = {}

        def ctx_of(i):
            order = ORDERS[i]
            axis = order[phase]
            base = {"x": ALL, "y": ALL, "z": ALL}
            for done in order[:phase]:
                base[done] = me[done]
            return axis, base

        def at_of(i, by):
            axis, base = ctx_of(i)
            return {**base, axis: lax.rem(me[axis] + by + 4, 4)}

        def ready(i, step):
            if phase == 0:
                for c in loads[i, step]:
                    c.wait()
                for c in pairs[i, step]:
                    c.wait_recv()
                add(i, at_of(i, TURN[step]), [(sib[i], True)])

        for i in range(n):
            axis, _ = ctx_of(i)
            b = bufs[12 * i + 4 * phase : 12 * i + 4 * phase + 4]
            s, r = send.at[i, phase], recv.at[i, phase]
            ready(i, 0)
            right, left = device_at(moved(me, axis, 1)), device_at(moved(me, axis, -1))
            far = at_of(i, 2)
            one = remote(view(work[i], wdims, far, (0, widths[i]), 0), b[0], s.at[0], r.at[0], right)
            two = remote(view(work[i], wdims, far, (0, widths[i]), 1), b[1], s.at[1], r.at[1], left)
            stage[i] = [b, s, r, right, left, one, two]
        for i in range(n):
            b, s, r, right, left, one, two = stage[i]
            ready(i, 1)
            one.wait_recv()
            add(i, at_of(i, 1), [(b[0], False)], 0)
            three = remote(view(work[i], wdims, at_of(i, 1), (0, widths[i])), b[2], s.at[2], r.at[2], right)
            ready(i, 2)
            two.wait_recv()
            add(i, at_of(i, -1), [(b[1], False)], 1)
            four = remote(view(work[i], wdims, at_of(i, -1), (0, widths[i])), b[3], s.at[3], r.at[3], left)
            stage[i] = [b, three, four]
            pending += [one, two, three, four]
        for i in range(n):
            b, three, four = stage[i]
            ready(i, 3)
            three.wait_recv()
            four.wait_recv()
            add(i, at_of(i, 0), [(b[2], False), (b[3], False)], None, out_ref if phase == 2 else None)
    for c in pending:
        c.wait_send()
    for k in pairs:
        for c in pairs[k]:
            c.wait_send()


def scatter(ins, dims, parts, rows, name, collective_id, vmem):
    n = len(parts)
    wdims = tuple(d for d in dims if d != "c")
    widths = [sum(width for _, (_, width), _ in sources) for sources in parts]
    wshape = tuple(SIZE[d] for d in wdims)
    dt = ins[0].dtype
    scratch = [pltpu.VMEM(wshape + (rows, w), dt) for w in widths] * 2
    for i in range(n):
        for phase in range(3):
            gone = set(ORDERS[i][: phase + 1])
            left = [d for d in wdims if ("z" if d in ("zh", "zl") else d) not in gone]
            shape = tuple(SIZE[d] for d in left)
            small = tuple(SIZE[d] for d in left if d != "l")
            halfw = widths[i] if "l" in dims else widths[i] // 2
            scratch += [pltpu.VMEM(small + (rows, halfw), dt)] * 2
            scratch += [pltpu.VMEM(shape + (rows, widths[i]), dt)] * 2
    most = max(len(s) for s in parts)
    scratch += [
        pltpu.SemaphoreType.DMA((n, 4, most)),
        pltpu.SemaphoreType.DMA((n, 4, most)),
        pltpu.SemaphoreType.DMA((n, 4, most)),
        pltpu.SemaphoreType.DMA((n, 3, 4)),
        pltpu.SemaphoreType.DMA((n, 3, 4)),
    ]
    lead = (2,) if "l" in dims else ()
    return pl.pallas_call(
        functools.partial(scatter_kernel, dims, parts, len(ins)),
        out_shape=jax.ShapeDtypeStruct(lead + (rows, sum(widths)), jnp.float32),
        in_specs=[pl.BlockSpec(memory_space=pl.ANY)] * len(ins),
        out_specs=pl.BlockSpec(memory_space=pltpu.VMEM),
        scratch_shapes=scratch,
        compiler_params=pltpu.CompilerParams(
            collective_id=collective_id, has_side_effects=True, vmem_limit_bytes=vmem
        ),
        name=name,
    )(*ins)


W_DIMS = ("zl", "zh", "x", "y", "c")
W_PARTS = ((0, 1792), (1792, 1792), (3584, 1792))
T_DIMS = ("l", "zh", "x", "y", "c", "zl")
T_PARTS = ((0, 256), (256, 256), (512, 128))


QH = 15
KEY_HEADS = 5
GROUPS = 3
HEAD_SIZE = 64
EPS = 1e-05
ROPE_BASE = 10000.0
NEGATIVE = -1e30
LOG2E = 1.4426950408889634
BLOCKS = 128
HALF = 64
SIDE = BLOCKS * HALF
LANES = GROUPS * HALF
CHUNK = 512
VMEM_LIMIT = 56 << 20


def chunk_ranges(side, own):
    count = SIDE // CHUNK
    if side == 0:
        diag = lax.div(HALF * own, CHUNK)
        first = HALF * (BLOCKS - own)
        edge, whole = lax.div(first, CHUNK), lax.div(first + CHUNK - 1, CHUNK)
        return ((diag, diag + 1), (0, diag)), ((edge, whole), (whole, count))
    rows = HALF * (own + 1)
    edge, whole = lax.div(rows, CHUNK), lax.div(rows + CHUNK - 1, CHUNK)
    diag = lax.div(HALF * (BLOCKS - 1 - own), CHUNK)
    return ((edge, whole), (0, edge)), ((diag, diag + 1), (diag + 1, count))


def seen(source, chunk, side, own):
    row = chunk * CHUNK + lax.broadcasted_iota(jnp.int32, (CHUNK, LANES), 0)
    block, place = row // HALF, row % HALF
    if source == 0:
        key = block * (2 * HALF) + place
    else:
        key = (BLOCKS - 1 - block) * (2 * HALF) + HALF + place
    col = lax.broadcasted_iota(jnp.int32, (CHUNK, LANES), 1)
    return key <= own * (2 * HALF) + side * HALF + col % HALF


def dot_nt(a, b):
    return lax.dot_general(a, b, (((1,), (1,)), ((), ())), preferred_element_type=jnp.float32)


def dot_tn(a, b):
    return lax.dot_general(a, b, (((0,), (0,)), ((), ())), preferred_element_type=jnp.float32)


def dot_nn(a, b):
    return lax.dot_general(a, b, (((1,), (0,)), ((), ())), preferred_element_type=jnp.float32)


def my_block():
    return lax.axis_index("ctx") * 2 + lax.axis_index("fsdp")


def attend_kernel(kv_ref, q_ref, o_ref, lse_ref, acc_ref):
    me = my_block()
    for side in range(2):
        own = me if side == 0 else BLOCKS - 1 - me
        q = q_ref[0, side]
        acc_ref[...] = jnp.zeros_like(acc_ref)
        carry = (jnp.full((1, LANES), NEGATIVE, jnp.float32), jnp.zeros((1, LANES), jnp.float32))

        def step(source, masked, chunk, carry):
            peak, total = carry
            kv = kv_ref[source, pl.ds(pl.multiple_of(chunk * CHUNK, CHUNK), CHUNK), :]
            s = dot_nt(kv, q) * LOG2E
            if masked:
                s = jnp.where(seen(source, chunk, side, own), s, NEGATIVE)
            new = jnp.maximum(peak, jnp.max(s, 0, keepdims=True))
            p = jnp.exp2(s - new)
            scale = jnp.exp2(peak - new)
            total = total * scale + jnp.sum(p, 0, keepdims=True)
            acc_ref[...] = acc_ref[...] * scale + dot_tn(kv, p.astype(jnp.bfloat16))
            return new, total

        for source, (edge, whole) in enumerate(chunk_ranges(side, own)):
            carry = lax.fori_loop(edge[0], edge[1], functools.partial(step, source, True), carry)
            carry = lax.fori_loop(whole[0], whole[1], functools.partial(step, source, False), carry)
        peak, total = carry
        o_ref[0, side] = acc_ref[HEAD_SIZE:, :] / total
        lse_ref[0, side] = peak + jnp.log2(total)


def attend(kv, q):
    return pl.pallas_call(
        attend_kernel,
        grid=(KEY_HEADS,),
        out_shape=(
            jax.ShapeDtypeStruct((KEY_HEADS, 2, HEAD_SIZE, LANES), jnp.float32),
            jax.ShapeDtypeStruct((KEY_HEADS, 2, 1, LANES), jnp.float32),
        ),
        in_specs=[
            pl.BlockSpec((2, SIDE, 128), lambda h: (0, 0, h)),
            pl.BlockSpec((1, 2, LANES, 128), lambda h: (h, 0, 0, 0)),
        ],
        out_specs=(
            pl.BlockSpec((1, 2, HEAD_SIZE, LANES), lambda h: (h, 0, 0, 0)),
            pl.BlockSpec((1, 2, 1, LANES), lambda h: (h, 0, 0, 0)),
        ),
        scratch_shapes=[pltpu.VMEM((128, LANES), jnp.float32)],
        compiler_params=pltpu.CompilerParams(vmem_limit_bytes=VMEM_LIMIT),
        name="attend",
    )(kv, q)


def attend_back_kernel(kv_ref, q_ref, do_ref, lse_ref, delta_ref, dq_ref, dkv_ref, acc_ref):
    me = my_block()
    dkv_ref[...] = jnp.zeros_like(dkv_ref)
    for side in range(2):
        own = me if side == 0 else BLOCKS - 1 - me
        q, do = q_ref[0, side], do_ref[0, side]
        lse, delta = lse_ref[0, side], delta_ref[0, side]
        acc_ref[...] = jnp.zeros_like(acc_ref)

        def step(source, masked, chunk, carry):
            rows = pl.ds(pl.multiple_of(chunk * CHUNK, CHUNK), CHUNK)
            kv = kv_ref[source, rows, :]
            p = jnp.exp2(dot_nt(kv, q) * LOG2E - lse)
            if masked:
                p = jnp.where(seen(source, chunk, side, own), p, 0.0)
            ds = (p * (dot_nt(kv, do) - delta)).astype(jnp.bfloat16)
            more = dot_nn(ds, q) + dot_nn(p.astype(jnp.bfloat16), do)
            dkv_ref[source, rows, :] = (dkv_ref[source, rows, :].astype(jnp.float32) + more).astype(jnp.bfloat16)
            acc_ref[...] += dot_tn(kv, ds)
            return carry

        for source, (edge, whole) in enumerate(chunk_ranges(side, own)):
            lax.fori_loop(edge[0], edge[1], functools.partial(step, source, True), 0)
            lax.fori_loop(whole[0], whole[1], functools.partial(step, source, False), 0)
        dq_ref[0, side] = acc_ref[:HEAD_SIZE, :]


def attend_back(kv, q, do, lse, delta):
    per_head = pl.BlockSpec((1, 2, LANES, 128), lambda h: (h, 0, 0, 0))
    row = pl.BlockSpec((1, 2, 1, LANES), lambda h: (h, 0, 0, 0))
    keys = pl.BlockSpec((2, SIDE, 128), lambda h: (0, 0, h))
    return pl.pallas_call(
        attend_back_kernel,
        grid=(KEY_HEADS,),
        out_shape=(
            jax.ShapeDtypeStruct((KEY_HEADS, 2, HEAD_SIZE, LANES), jnp.float32),
            jax.ShapeDtypeStruct(kv.shape, jnp.bfloat16),
        ),
        in_specs=[keys, per_head, per_head, row, row],
        out_specs=(pl.BlockSpec((1, 2, HEAD_SIZE, LANES), lambda h: (h, 0, 0, 0)), keys),
        scratch_shapes=[pltpu.VMEM((128, LANES), jnp.float32)],
        compiler_params=pltpu.CompilerParams(vmem_limit_bytes=VMEM_LIMIT),
        name="attend_back",
    )(kv, q, do, lse, delta)


def rotary_tables(positions):
    half = HEAD_SIZE // 2
    freq = ROPE_BASE ** (-(jnp.arange(half, dtype=jnp.float32) * 2.0 / HEAD_SIZE))
    angle = positions.astype(jnp.float32)[:, None] * freq[None, :]
    return (jnp.cos(angle)[:, None, :], jnp.sin(angle)[:, None, :])


def rotate(values, cosine, sine):
    count = values.shape[0]
    half = HEAD_SIZE // 2
    heads = values.reshape(count, -1, HEAD_SIZE)
    first = heads[..., :half]
    second = heads[..., half:]
    return jnp.concatenate(
        [first * cosine - second * sine, second * cosine + first * sine], -1
    ).reshape(count, -1)


def mm(form, left, right):
    return jnp.einsum(form, left, right, preferred_element_type=jnp.float32)


def by_head(rows):
    r = rows.reshape(2, HALF, KEY_HEADS, GROUPS, HEAD_SIZE)
    return jnp.transpose(r, (2, 0, 3, 1, 4)).reshape(KEY_HEADS, 2, LANES, HEAD_SIZE)


def by_token(heads):
    h = heads.reshape(KEY_HEADS, 2, HEAD_SIZE, GROUPS, HALF)
    return jnp.transpose(h, (1, 4, 0, 3, 2)).reshape(2 * HALF, QH * HEAD_SIZE)


def local(
    layer_in,
    attn_gain,
    query_weight,
    key_weight,
    value_weight,
    output_weight,
    ffn_gain,
    gate_weight,
    up_weight,
    down_weight,
    out_cotangent,
):
    bf, f32 = jnp.bfloat16, jnp.float32
    me = my_block()
    swap = [(i, BLOCKS - 1 - i) for i in range(BLOCKS)]

    def exchanged(rows):
        return lax.ppermute(rows, ("ctx", "fsdp"), swap)

    both = jnp.concatenate([layer_in, out_cotangent], 1)
    both = jnp.concatenate([both[:HALF], exchanged(both[HALF:])], 0)
    x_low, dy = both[:, :960], both[:, 960:]

    down = jnp.zeros((48, 512), bf)
    down = down.at[:40, :480].set(down_weight)
    down = down.at[40, :15].set(attn_gain).at[41, :15].set(ffn_gain)
    down = down.reshape(3, 16, 512)
    qkvo = jnp.concatenate([query_weight, key_weight, value_weight, output_weight], 1)
    mats = [jnp.pad(a, ((0, 1), (0, 0))) for a in (gate_weight, up_weight, qkvo)]
    piece = jnp.concatenate([a for i in range(3) for a in (mats[i], down[i])], 1)
    whole = gather(piece, W_DIMS, W_PARTS, "gather_weights", 1).reshape(2, 64, 16, 5376)
    flat = whole.reshape(2, 1024, 5376)
    w_gate, w_up = flat[:, :, :1280], flat[:, :, 1792:3072]
    w_qkv, w_out = flat[:, :, 3584:4384], flat[:, :, 4384:4864]
    w_down = jnp.stack([whole[..., 1280:1792], whole[..., 3072:3584], whole[..., 4864:5376]], 2)
    w_down = w_down.reshape(2, 64, 48, 512)[:, :, :40, :480].reshape(2, 2560, 480)
    gain_one = whole[0, :, 8, 4864:4880].reshape(1024).astype(f32)
    gain_two = whole[0, :, 9, 4864:4879].reshape(960).astype(f32)

    i = lax.broadcasted_iota(jnp.int32, (960, 1024), 0)
    j = lax.broadcasted_iota(jnp.int32, (960, 1024), 1)
    spread = (j == (i // 15) * 16 + i % 15).astype(bf)

    def wide(rows):
        return mm("td,de->te", rows, spread)

    def narrow_low(rows):
        return mm("te,de->td", rows, spread)

    def narrow(rows):
        high = rows.astype(bf)
        rest = rows - high.astype(f32)
        middle = rest.astype(bf)
        last = (rest - middle.astype(f32)).astype(bf)
        return narrow_low(high) + narrow_low(middle) + narrow_low(last)

    t = jnp.arange(HALF, dtype=jnp.int32)
    positions = jnp.concatenate([me * 128 + t, (BLOCKS - 1 - me) * 128 + HALF + t])
    cosine, sine = rotary_tables(positions)

    hidden = wide(x_low)
    factor_one = lax.rsqrt(jnp.sum(hidden * hidden, -1, keepdims=True) / 960 + EPS)
    normed = (hidden * factor_one * gain_one).astype(bf)
    qkv = mm("te,hec->thc", normed, w_qkv)
    query = qkv[:, :, :480].reshape(128, 960)
    key = qkv[:, :, 480:640].reshape(128, 320)
    value = qkv[:, :, 640:800].reshape(128, 320)
    query_rot = rotate(query, cosine, sine).astype(bf)
    key_rot = rotate(key, cosine, sine).astype(bf)
    kv_piece = jnp.concatenate(
        [key_rot.reshape(2, HALF, KEY_HEADS, 64), value.astype(bf).reshape(2, HALF, KEY_HEADS, 64)], -1
    ).reshape(2, HALF, 640)
    kv = gather(kv_piece, T_DIMS, T_PARTS, "gather_keys", 2).reshape(2, SIDE, 640)
    q_heads = jnp.pad(by_head(query_rot * jnp.asarray(0.125, bf)), ((0, 0), (0, 0), (0, 0), (0, 64)))
    attn_heads, lse = attend(kv, q_heads)
    attn = by_token(attn_heads)
    attn_low = attn.astype(bf)
    attn_wide = wide(attn_low).astype(bf)
    middle = x_low.astype(f32) + mm("te,hec->thc", attn_wide, w_out).reshape(128, 960)
    factor_two = lax.rsqrt(jnp.mean(middle * middle, -1, keepdims=True) + EPS)
    normed_two = wide((middle * factor_two * gain_two).astype(bf)).astype(bf)
    gate = mm("te,hec->thc", normed_two, w_gate)
    upward = mm("te,hec->thc", normed_two, w_up)
    sigma = jax.nn.sigmoid(gate)
    activated = gate * sigma
    inner = (activated * upward).astype(bf)
    inner_flat = inner.reshape(128, 2560)
    layer_out = (middle + mm("tf,hfd->thd", inner_flat, w_down).reshape(128, 960)).astype(bf)
    layer_out = jnp.concatenate([layer_out[:HALF], exchanged(layer_out[HALF:])], 0)

    dy_split = dy.reshape(128, 2, 480)
    inner_grad = mm("thd,hfd->tf", dy_split, w_down).reshape(128, 2, 1280)
    gate_low = (inner_grad * upward * sigma * (1.0 + gate * (1.0 - sigma))).astype(bf)
    up_low = (inner_grad * activated).astype(bf)
    down_term = mm("tf,thd->hfd", inner_flat, dy_split).astype(bf)
    gate_term = mm("te,thc->hec", normed_two, gate_low).astype(bf)
    up_term = mm("te,thc->hec", normed_two, up_low).astype(bf)
    grad_two = narrow(mm("thc,hec->te", gate_low, w_gate) + mm("thc,hec->te", up_low, w_up))
    weighted = gain_two * grad_two
    middle_grad = dy.astype(f32) + (
        factor_two * weighted - middle * factor_two**3 * jnp.mean(weighted * middle, -1, keepdims=True)
    )
    gain_two_term = jnp.sum(grad_two * middle * factor_two, 0)
    middle_low = middle_grad.astype(bf)
    out_term = mm("te,thd->hed", attn_wide, middle_low.reshape(128, 2, 480)).astype(bf)
    attn_grad = narrow_low(mm("thd,hed->te", middle_low.reshape(128, 2, 480), w_out).astype(bf)).astype(bf)
    delta = jnp.sum((attn_grad.astype(f32) * attn).reshape(2, HALF, KEY_HEADS, GROUPS, HEAD_SIZE), -1)
    delta = jnp.transpose(delta, (2, 0, 3, 1)).reshape(KEY_HEADS, 2, 1, LANES)
    do_heads = jnp.pad(by_head(attn_grad), ((0, 0), (0, 0), (0, 0), (64, 0)))
    dq_heads, dkv = attend_back(kv, q_heads, do_heads, lse, delta)
    dkv = dkv.reshape(2, 2, 4, 4, 2, 2, HALF, 640)
    parts = tuple(((0, c, 0),) for c in T_PARTS)
    key_sums = scatter([dkv], T_DIMS, parts, HALF, "scatter_keys", 3, VMEM_LIMIT)
    key_sums = key_sums.reshape(128, KEY_HEADS, 128)
    query_low = rotate(by_token(dq_heads) * 0.125, cosine, -sine).astype(bf)
    key_low = rotate(key_sums[..., :64].reshape(128, 320), cosine, -sine).astype(bf)
    value_low = key_sums[..., 64:].reshape(128, 320).astype(bf)
    qkv_low = jnp.concatenate(
        [query_low.reshape(128, 2, 480), key_low.reshape(128, 2, 160), value_low.reshape(128, 2, 160)], -1
    )
    qkv_term = mm("te,thc->hec", normed, qkv_low).astype(bf)
    normed_grad = mm("thc,hec->te", qkv_low, w_qkv)
    weighted = gain_one * normed_grad
    input_back = factor_one * weighted - hidden * factor_one**3 * (
        jnp.sum(weighted * hidden, -1, keepdims=True) / 960
    )
    gain_one_term = jnp.sum(normed_grad * hidden * factor_one, 0)
    input_grad = middle_grad + narrow(input_back)
    input_grad = jnp.concatenate([input_grad[:HALF], exchanged(input_grad[HALF:])], 0)

    qkvo_term = jnp.concatenate([qkv_term, out_term], -1)
    down_pad = jnp.pad(down_term.reshape(2, 64, 40, 480), ((0, 0), (0, 0), (0, 0), (0, 32)))
    gains = jnp.stack(
        [gain_one_term.reshape(64, 16)[:, :15], gain_two_term.reshape(64, 15)], 1
    ).astype(bf)
    gains = jnp.pad(gains, ((0, 0), (0, 6), (0, 512 - 15)))
    down_pad = jnp.concatenate([down_pad, jnp.broadcast_to(gains, (2, 64, 8, 512))], 2)
    down_pad = jnp.transpose(down_pad.reshape(2, 64, 3, 16, 512), (0, 1, 3, 2, 4)).reshape(2, 64, 16, 1536)
    terms = [gate_term, up_term, qkvo_term, down_pad]
    terms = [lax.optimization_barrier(a).reshape(2, 2, 4, 4, 2, 16, -1) for a in terms]
    parts = tuple(((k, (0, 1280), 0), (3, (512 * k, 512), 1280)) for k in range(3))
    sums = scatter(terms, W_DIMS, parts, 16, "scatter_weights", 4, VMEM_LIMIT)
    down_sum = jnp.concatenate([sums[:, 1280:1792], sums[:, 3072:3584], sums[:, 4864:5376]], 0)
    return (
        layer_out,
        input_grad,
        down_sum[40, :15],
        sums[:15, 3584:4064],
        sums[:15, 4064:4224],
        sums[:15, 4224:4384],
        sums[:15, 4384:4864],
        down_sum[41, :15],
        sums[:15, :1280],
        sums[:15, 1792:3072],
        down_sum[:40, :480],
    )


def solution(mesh):
    matrix, tokens = P("ctx", "fsdp"), P(("ctx", "fsdp"), None)
    return jax.shard_map(
        local,
        mesh=mesh,
        in_specs=(tokens, P("ctx"), matrix, matrix, matrix, matrix, P("ctx"), matrix, matrix, matrix, tokens),
        out_specs=(tokens, tokens, P("ctx"), matrix, matrix, matrix, matrix, P("ctx"), matrix, matrix, matrix),
        check_vma=False,
    )
```

time: 1960 us -> 694 us (0.35)
  waiting for transfers between devices: 996 us -> 6.53 us
  Pallas kernels: 0 us -> 480 us
  matrix products: 384 us -> 63.9 us
  blocking collectives: 173 us -> 0 us
  local copies, waits for them, and re-layouts: 232 us -> 91.2 us
  other arithmetic: 113 us -> 21.7 us
    reduce_scatter x2 -> x0, waiting for transfers between devices: 491 us -> none  [the longest x1 360 us: sum_packed(): lax.psum_scatter(lines, axis, tiled=True).reshape(-1)]
    pallas_call x0 -> x6, Pallas kernels: none -> 480 us  [the longest x2 145 us: scatter(): pl.pallas_call(functools.partial(scatter_kernel, dims, parts, len(ins)),...]
    dot_general x28 -> x24, matrix products: 384 us -> 63.9 us  [mm(): return jnp.einsum(form, left, right, preferred_element_type=jnp.float32)]
    all_gather x8 -> x0, waiting for transfers between devices: 275 us -> none  [the longest x3 132 us: in_one_piece(): out = lax.all_gather(both, axis, axis=dim, tiled=True)]
    all_to_all x7 -> x0, waiting for transfers between devices: 229 us -> none  [summed_on_arrival(): parts = lax.all_to_all(in_blocks(x, dim, count), axis, 0, 0, tiled=True)]
    unnamed x1 -> x0, blocking collectives: 167 us -> none
    unnamed x99 -> x109, local copies, waits for them, and re-layouts: 76.2 us -> 5.2 us
    reduce_sum x10 -> x2, other arithmetic: 62.1 us -> 0.61 us  [the longest x1 0.39 us: local(): jnp.sum((attn_grad.astype(f32) * attn).reshape(2, HALF, KEY_HEADS, GROUPS...]
  transfers between devices with their start and end apart: 17 -> 3, of which waited for: 11 -> 1; matrix products, arithmetic and copies ran while one was open for 16% -> 6% of each run, Pallas kernels for 0% -> 9%
where the time goes in v1:
time: 694 us; the launch traced here: 681 us
  Pallas kernels  480 us (69%)
  local copies, waits for them, and re-layouts  91.2 us (13%)
  matrix products  63.9 us (9%)
  other arithmetic  21.7 us (3%)
  starting transfers between devices  15.8 us (2%)
    pallas_call x2, Pallas kernels, scatter(): pl.pallas_call(functools.partial(scatter_kernel, dims, parts, len(ins)),...  145 us
    pallas_call x2, Pallas kernels, gather(): pl.pallas_call(functools.partial(gather_kernel, dims, parts), out_shape=j...  133 us
    pallas_call x1, Pallas kernels, attend_back(): pl.pallas_call(attend_back_kernel, grid=(KEY_HEADS,), out_shape=(jax.Shap...  106 us
    pallas_call x1, Pallas kernels, attend(): pl.pallas_call(attend_kernel, grid=(KEY_HEADS,), out_shape=(jax.ShapeDtyp...  95.8 us
    dot_general x24, matrix products, mm(): return jnp.einsum(form, left, right, preferred_element_type=jnp.float32)  63.9 us
    optimization_barrier x3, local copies, waits for them, and re-layouts, local(): lax.optimization_barrier(a).reshape(2, 2, 4, 4, 2, 16, -1)  23.9 us
    ppermute x3, starting transfers between devices, exchanged(): return lax.ppermute(rows, ('ctx', 'fsdp'), swap)  15.8 us
  transfers between devices with their start and end apart: 3, of which 1 were waited for; matrix products, arithmetic and copies ran while one was open for 6% of the time, Pallas kernels for 9%

profile of v1, /device:TPU:0, one launch (start us, length us, event | category | flops | bytes accessed | tf_op | source)
XLA Modules:
  0.0 680.8 jit_solution(11368259663572445357)
XLA Ops:
  3.6 8.2 %collective-permute-start = (bf16[64,1920]{0,1:T(8,128)(2,1)}, bf16[64,1920]{0,1:T(8,128)(2,1)S(1)}, u32[]{:S(2)}, u32[]{:S(2)}) collective-permute-start(bf16[64,1920]{0,1:T(8,128)(2,1)} %get-tuple-element.77), channel_id=1, source_target_pairs={{0,127},{1,126},{2,125},{3,124},{4,123},{5,122},{6,121},{7,120},{8... | collective-permute-start | bytes 737288 | tf_op jit(solution)/shard_map/ppermute | solution.py:571
  17.3 64.0 %gather_weights.1 = bf16[2,2,4,4,2,16,5376]{6,5,4,3,2,1,0:T(8,128)(2,1)} custom-call(bf16[16,5376]{1,0:T(8,128)(2,1)} %copy-done.16), custom_call_target="tpu_custom_call" | custom-call | tf_op jit(solution)/shard_map/gather_weights/pallas_call | solution.py:139
  82.3 6.0 slice_bitcast_fusion.2
  89.6 5.5 pad_maximum_fusion
  95.4 5.2 slice.273
  100.5 7.7 %copy.90 = bf16[2,2560,480]{1,2,0:T(8,128)(2,1)} copy(bf16[2,2560,480]{2,1,0:T(8,128)(2,1)} %bitcast.163) | data formatting | bytes 9830400 | tf_op jit(solution)/shard_map/reshape | solution.py:589
  110.0 2.4 multiply_reduce_fusion.2
  112.9 3.6 fusion.16
  119.2 68.9 %gather_keys.1 = bf16[2,2,4,4,2,2,64,640]{7,6,5,4,3,2,1,0:T(8,128)(2,1)} custom-call(bf16[2,64,640]{2,1,0:T(8,128)(2,1)} %reshape.379.piece_ref), custom_call_target="tpu_custom_call" | custom-call | tf_op jit(solution)/shard_map/gather_keys/pallas_call | solution.py:139
  190.5 95.8 %attend.1 = (f32[5,2,64,192]{3,2,1,0:T(8,128)}, f32[5,2,1,192]{3,2,1,0:T(1,128)}) custom-call(bf16[2,8192,640]{2,1,0:T(8,128)(2,1)} %bitcast.140, bf16[5,2,192,128]{3,2,1,0:T(8,128)(2,1)} %pad.41.q_ref), custom_call_target="tpu_custom_call" | custom-call | tf_op jit(solution)/shard_map/attend/pallas_call | solution.py:454
  286.3 1.4 copy.84
  290.7 3.7 fusion.23
  294.7 1.4 fusion.49
  296.1 3.5 fusion.12
  299.6 3.4 fusion.8
  303.2 2.2 multiply_convert_fusion
  305.5 4.3 fusion.34
  309.8 3.8 fusion.14
  313.6 3.8 fusion.15
  317.4 4.7 fusion.41
  323.4 1.3 convolution_add_fusion.3
  324.7 2.0 multiply_reduce_fusion.3
  327.3 4.0 convert_multiply_fusion
  331.4 2.0 convert_bitcast_fusion.1
  337.4 106.1 %attend_back.1 = (f32[5,2,64,192]{3,2,1,0:T(8,128)}, bf16[2,8192,640]{2,1,0:T(8,128)(2,1)}) custom-call(bf16[2,8192,640]{2,1,0:T(8,128)(2,1)} %bitcast.141, bf16[5,2,192,128]{3,2,1,0:T(8,128)(2,1)} %pad.41.q_ref, bf16[5,2,192,128]{3,2,1,0:T(8,128)(2,1)} %pad.42.do_ref, f32[5,2,1,192]{3,2,1,0:T(1,128)} %get-tuple-element.52.lse_ref, ...), custom_call_target="tpu_custom_call" | custom-call | tf_op jit(solution)/shard_map/attend_back/pallas_call | solution.py:506
  443.5 79.7 %scatter_keys.1 = f32[2,64,640]{2,1,0:T(8,128)} custom-call(bf16[2,2,4,4,2,2,64,640]{7,6,5,4,3,2,1,0:T(8,128)(2,1)} %bitcast.164), custom_call_target="tpu_custom_call" | custom-call | tf_op jit(solution)/shard_map/scatter_keys/pallas_call | solution.py:349
  529.7 4.2 multiply_reduce_fusion
  533.9 2.1 convert_bitcast_fusion
  536.1 2.2 copy.87
  538.2 7.9 %copy.103 = bf16[2,1024,1280]{2,1,0:T(8,128)(2,1)} copy(bf16[2,1024,1280]{1,2,0:T(8,128)(2,1)} %fusion.14) | data formatting | bytes 10485760 | tf_op jit(solution)/shard_map/optimization_barrier | solution.py:693
  546.1 8.1 %copy.105 = bf16[2,1024,1280]{2,1,0:T(8,128)(2,1)} copy(bf16[2,1024,1280]{1,2,0:T(8,128)(2,1)} %fusion.15) | data formatting | bytes 10485760 | tf_op jit(solution)/shard_map/optimization_barrier | solution.py:693
  554.2 4.5 pad_maximum_fusion.1
  558.6 7.9 %copy.106 = bf16[2,1024,1280]{2,1,0:T(8,128)(2,1)} copy(bf16[2,1024,1280]{1,2,0:T(8,128)(2,1)} %pad_maximum_fusion.1) | data formatting | bytes 10485760 | tf_op jit(solution)/shard_map/optimization_barrier | solution.py:693
  566.6 3.7 fusion.5
  570.3 7.9 %copy.108 = bf16[2,2560,480]{2,1,0:T(8,128)(2,1)} copy(bf16[2,2560,480]{1,2,0:T(8,128)(2,1)} %fusion.5) | data formatting | bytes 9830400 | tf_op jit(solution)/shard_map/convert_element_type | solution.py:648
  578.9 3.6 fusion.1
  582.6 3.5 copy.125
  586.0 65.1 %scatter_weights.1 = f32[16,5376]{1,0:T(8,128)} custom-call(bf16[2,2,4,4,2,16,1280]{6,5,4,3,2,1,0:T(8,128)(2,1)} %bitcast.165, bf16[2,2,4,4,2,16,1280]{6,5,4,3,2,1,0:T(8,128)(2,1)} %bitcast.166, bf16[2,2,4,4,2,16,1280]{6,5,4,3,2,1,0:T(8,128)(2,1)} %bitcast.167, bf16[2,2,4,4,2,16,1536]{6,5,4,3,2,1,0:T(8,128)(2,1)} %bitcast.154), custom_call_target="tpu_custom_call" | custom-call | tf_op jit(solution)/shard_map/scatter_weights/pallas_call | solution.py:349
  651.2 1.5 fusion.85
  652.6 1.5 fusion.86
  654.1 1.6 fusion.84
  656.7 1.4 fusion.47
  658.9 1.3 fusion.57
  660.2 1.3 convolution_add_fusion.1
  661.6 1.3 fusion.40
  663.1 7.2 %collective-permute-start.2 = (f32[64,960]{0,1:T(8,128)S(1)}, f32[64,960]{0,1:T(8,128)S(1)}, u32[]{:S(2)}, u32[]{:S(2)}) collective-permute-start(f32[64,960]{0,1:T(8,128)S(1)} %get-tuple-element.76), channel_id=1, source_target_pairs={{0,127},{1,126},{2,125},{3,124},{4,123},{5,122},{6,121},{7,120},{8... | collective-permute-start | bytes 737288 | tf_op jit(solution)/shard_map/ppermute | solution.py:571
  670.3 1.3 slice_bitcast_fusion.3
  673.0 6.5 collective-permute-done.2
  (198 shorter events, 38.6 us)
Async XLA Ops:
  3.6 105.6 %collective-permute-start = (bf16[64,1920]{0,1:T(8,128)(2,1)}, bf16[64,1920]{0,1:T(8,128)(2,1)S(1)}, u32[]{:S(2)}, u32[]{:S(2)}) collective-permute-start(bf16[64,1920]{0,1:T(8,128)(2,1)} %get-tuple-element.77), channel_id=1, source_target_pairs={{0,127},{1,126},{2,125},{3,124},{4,123},{5,122},{6,121},{7,120},{8... | collective-permute-start | bytes 737288 | tf_op jit(solution)/shard_map/ppermute | solution.py:571
  95.1 229.6 %copy-start.35 = (pred[960]{0:T(1024)(128)(4,1)}, pred[960]{0:T(1024)(128)(4,1)S(1)}, u32[]{:S(2)}) copy-start(pred[960]{0:T(1024)(128)(4,1)S(1)} %get-tuple-element.111) | copy-start | bytes 2884
  95.1 229.6 %copy-start.37 = (pred[960]{0:T(1024)(128)(4,1)}, pred[960]{0:T(1024)(128)(4,1)S(1)}, u32[]{:S(2)}) copy-start(pred[960]{0:T(1024)(128)(4,1)S(1)} %get-tuple-element.112) | copy-start | bytes 2884
  95.2 17.8 %copy-start.18 = (f32[1024]{0:T(1024)}, f32[1024]{0:T(1024)S(1)}, u32[]{:S(2)}) copy-start(f32[1024]{0:T(1024)S(1)} %reshape.404) | copy-start | bytes 12292
  95.4 22.1 %copy-start.8 = (f32[128,32]{1,0:T(8,128)}, f32[128,32]{1,0:T(8,128)S(1)}, u32[]{:S(2)}) copy-start(f32[128,32]{1,0:T(8,128)S(1)} %copy.76) | copy-start | bytes 49156
  108.4 218.3 %copy-start.21 = (f32[960]{0:T(1024)}, f32[960]{0:T(1024)S(1)}, u32[]{:S(2)}) copy-start(f32[960]{0:T(1024)S(1)} %reshape.405) | copy-start | bytes 11524
  109.1 215.5 %copy-start.23 = (s32[960]{0:T(1024)}, s32[960]{0:T(1024)S(1)}, u32[]{:S(2)}) copy-start(s32[960]{0:T(1024)S(1)} %get-tuple-element.107) | copy-start | bytes 11524
  109.1 215.5 %copy-start.25 = (s32[960]{0:T(1024)}, s32[960]{0:T(1024)S(1)}, u32[]{:S(2)}) copy-start(s32[960]{0:T(1024)S(1)} %get-tuple-element.108) | copy-start | bytes 11524
  109.1 215.5 %copy-start.27 = (s32[960]{0:T(1024)}, s32[960]{0:T(1024)S(1)}, u32[]{:S(2)}) copy-start(s32[960]{0:T(1024)S(1)} %get-tuple-element.109) | copy-start | bytes 11524
  109.2 215.5 %copy-start.29 = (s32[960]{0:T(1024)}, s32[960]{0:T(1024)S(1)}, u32[]{:S(2)}) copy-start(s32[960]{0:T(1024)S(1)} %get-tuple-element.110) | copy-start | bytes 11524
  112.3 417.3 %copy-start.3 = (f32[128,1024]{1,0:T(8,128)}, f32[128,1024]{1,0:T(8,128)S(1)}, u32[]{:S(2)}) copy-start(f32[128,1024]{1,0:T(8,128)S(1)} %get-tuple-element.102) | copy-start | bytes 1572868
  112.9 4.3 copy-start.31
  289.5 4.9 copy-start.13
  289.5 4.9 copy-start.6
  294.6 32.0 %copy-start.1 = (f32[128,960]{0,1:T(8,128)}, f32[128,960]{0,1:T(8,128)S(1)}, u32[]{:S(2)}) copy-start(f32[128,960]{0,1:T(8,128)S(1)} %get-tuple-element.60) | copy-start | bytes 1474564
  294.7 32.0 %copy-start.40 = (f32[128]{0:T(128)}, f32[128]{0:T(128)S(1)}, u32[]{:S(2)}) copy-start(f32[128]{0:T(128)S(1)} %get-tuple-element.99) | copy-start | bytes 1540
  294.7 32.0 %copy-start.42 = (f32[128]{0:T(128)}, f32[128]{0:T(128)S(1)}, u32[]{:S(2)}) copy-start(f32[128]{0:T(128)S(1)} %get-tuple-element.100) | copy-start | bytes 1540
  296.1 7.1 %slice-start = ((s8[4915200]{0:T(1024)(128)(4,1)}), s8[4194304]{0:T(1024)(128)(4,1)S(1)}, s32[]{:S(2)}) async-start(s8[4915200]{0:T(1024)(128)(4,1)} %bitcast.156), calls=%async_computation | async-start | bytes 8388608
  299.6 3.6 slice-start.1
  324.7 2.6 copy-start.14
  326.7 4.7 copy-start.11
  443.5 81.7 %copy-start.9 = (f32[128,32]{1,0:T(8,128)S(1)}, f32[128,32]{1,0:T(8,128)}, u32[]{:S(2)}) copy-start(f32[128,32]{1,0:T(8,128)} %copy-done.8) | copy-start | bytes 49156
  443.5 81.7 %copy-start.17 = (f32[128,32]{1,0:T(8,128)S(1)}, f32[128,32]{1,0:T(8,128)}, u32[]{:S(2)}) copy-start(f32[128,32]{1,0:T(8,128)} %copy.98) | copy-start | bytes 49156
  523.2 3.3 copy-start.7
  526.5 3.2 copy-start.19
  526.5 3.2 copy-start.32
  528.8 5.2 copy-start.15
  528.8 5.1 copy-start.20
  528.8 5.1 copy-start.33
  558.6 7.9 %copy-start = (bf16[128,2,1280]{0,2,1:T(8,128)(2,1)S(1)}, bf16[128,2,1280]{0,2,1:T(8,128)(2,1)}, u32[]{:S(2)}) copy-start(bf16[128,2,1280]{0,2,1:T(8,128)(2,1)} %copy.87) | copy-start | bytes 1966084
  570.3 7.9 %copy-start.34 = (bf16[960]{0:T(1024)(128)(2,1)S(1)}, bf16[960]{0:T(1024)(128)(2,1)}, u32[]{:S(2)}) copy-start(bf16[960]{0:T(1024)(128)(2,1)} %get-tuple-element.57) | copy-start | bytes 5764
  582.6 74.0 %slice-start.2 = ((s8[4915200]{0:T(1024)(128)(4,1)}), s8[4194304]{0:T(1024)(128)(4,1)S(1)}, s32[]{:S(2)}) async-start(s8[4915200]{0:T(1024)(128)(4,1)} %bitcast.159), calls=%async_computation.2 | async-start | bytes 8388608
  586.0 70.6 %slice-start.3 = ((s8[4915200]{0:T(1024)(128)(4,1)}), s8[720896]{0:T(1024)(128)(4,1)S(1)}, s32[]{:S(2)}) async-start(s8[4915200]{0:T(1024)(128)(4,1)} %bitcast.159), calls=%async_computation.3 | async-start | bytes 1441792
  586.0 70.6 %copy-start.2 = (f32[128,960]{0,1:T(8,128)S(1)}, f32[128,960]{0,1:T(8,128)}, u32[]{:S(2)}) copy-start(f32[128,960]{0,1:T(8,128)} %copy-done.1) | copy-start | bytes 1474564
  655.7 2.9 copy-start.4
  655.7 2.9 copy-start.10
  655.7 3.0 copy-start.39
  656.6 2.2 copy-start.24
  656.7 2.2 copy-start.26
  656.7 2.2 copy-start.28
  656.7 2.2 copy-start.30
  656.7 2.2 copy-start.36
  656.7 2.2 copy-start.38
  658.3 13.9 %collective-permute-start.1 = (bf16[64,960]{0,1:T(8,128)(2,1)S(1)}, bf16[64,960]{0,1:T(8,128)(2,1)S(1)}, u32[]{:S(2)}, u32[]{:S(2)}) collective-permute-start(bf16[64,960]{0,1:T(8,128)(2,1)S(1)} %get-tuple-element.91), channel_id=1, source_target_pairs={{0,127},{1,126},{2,125},{3,124},{4,123},{5,122},{6,121},{7,120},{8... | collective-permute-start | bytes 368648 | tf_op jit(solution)/shard_map/ppermute | solution.py:571
  660.2 1.3 copy-start.12
  660.2 1.3 copy-start.22
  660.2 1.3 copy-start.41
  663.1 16.5 %collective-permute-start.2 = (f32[64,960]{0,1:T(8,128)S(1)}, f32[64,960]{0,1:T(8,128)S(1)}, u32[]{:S(2)}, u32[]{:S(2)}) collective-permute-start(f32[64,960]{0,1:T(8,128)S(1)} %get-tuple-element.76), channel_id=1, source_target_pairs={{0,127},{1,126},{2,125},{3,124},{4,123},{5,122},{6,121},{7,120},{8... | collective-permute-start | bytes 737288 | tf_op jit(solution)/shard_map/ppermute | solution.py:571
  (5 other events, 4.8 us)

commit v2 on v1

--- a/solution.py
+++ b/solution.py
@@ -33,12 +33,36 @@
     return {**at, axis: lax.rem(at[axis] + by + size, size)}
 
 
+def mirror():
+    return (63 - lax.axis_index("ctx"), 1 - lax.axis_index("fsdp"))
+
+
 def greet(me):
     barrier = pltpu.get_barrier_semaphore()
     others = [moved(me, a, s) for a in "xyz" for s in (1, -1)] + [moved(me, "c", 1)]
-    for other in others:
-        pl.semaphore_signal(barrier, inc=1, device_id=device_at(other), device_id_type=MESH)
-    pl.semaphore_wait(barrier, len(others))
+    targets = [device_at(other) for other in others] + [mirror()]
+    for target in targets:
+        pl.semaphore_signal(barrier, inc=1, device_id=target, device_id_type=MESH)
+    pl.semaphore_wait(barrier, len(targets))
+
+
+def start_trades(pairs, sems):
+    out = []
+    for k, (src, dst) in enumerate(pairs):
+        half = src.shape[0] // 2
+        stay = pltpu.make_async_copy(src.at[pl.ds(0, half)], dst.at[pl.ds(0, half)], sems.at[k, 0])
+        go = pltpu.make_async_remote_copy(
+            src_ref=src.at[pl.ds(half, half)],
+            dst_ref=dst.at[pl.ds(half, half)],
+            send_sem=sems.at[k, 1],
+            recv_sem=sems.at[k, 2],
+            device_id=mirror(),
+            device_id_type=MESH,
+        )
+        stay.start()
+        go.start()
+        out += [stay, go]
+    return out
 
 
 def place(dims, at):
@@ -54,21 +78,23 @@
     return index
 
 
-def view(ref, dims, at, cols, half=None):
+def view(ref, dims, at, cols, half=None, rows=ALL):
     start, width = cols
     if half is not None:
         if "l" in dims:
             at = {**at, "l": half}
         else:
             start, width = start + half * (width // 2), width // 2
-    return ref.at[tuple(place(dims, at)) + (ALL, pl.ds(start, width))]
-
-
-def gather_kernel(dims, parts, piece_ref, out_ref, send, recv, sib_send, sib_recv, own_sem):
+    return ref.at[tuple(place(dims, at)) + (rows, pl.ds(start, width))]
+
+
+def gather_kernel(dims, parts, trades, *refs):
+    piece_ref, out_ref = refs[0], refs[1 + trades]
+    send, recv, sib_send, sib_recv, own_sem, trade_sem = refs[2 + 2 * trades :]
     me = whereabouts()
     greet(me)
+    swaps = start_trades(list(zip(refs[1 : 1 + trades], refs[2 + trades : 2 + 2 * trades])), trade_sem)
     sibling = device_at(moved(me, "c", 1))
-    lead = (ALL,) if "l" in dims else ()
 
     def copy(src, dst, ssem, rsem, to):
         c = pltpu.make_async_remote_copy(
@@ -128,37 +154,45 @@
                     c.wait_recv()
     for c in pending:
         c.wait_send()
+    for c in swaps:
+        c.wait()
 
 
 SIZE = {"zl": 2, "zh": 2, "x": 4, "y": 4, "c": 2, "l": 2}
 
 
-def gather(piece, dims, parts, name, collective_id):
+def gather(piece, dims, parts, name, collective_id, trades=()):
     shape = tuple(SIZE[d] for d in dims) + piece.shape[-2:]
     n = len(parts)
+    anywhere = pl.BlockSpec(memory_space=pl.ANY)
     return pl.pallas_call(
-        functools.partial(gather_kernel, dims, parts),
-        out_shape=jax.ShapeDtypeStruct(shape, piece.dtype),
-        in_specs=[pl.BlockSpec(memory_space=pl.ANY)],
-        out_specs=pl.BlockSpec(memory_space=pl.ANY),
+        functools.partial(gather_kernel, dims, parts, len(trades)),
+        out_shape=(
+            jax.ShapeDtypeStruct(shape, piece.dtype),
+            *(jax.ShapeDtypeStruct(t.shape, t.dtype) for t in trades),
+        ),
+        in_specs=[anywhere] * (1 + len(trades)),
+        out_specs=(anywhere,) * (1 + len(trades)),
         scratch_shapes=[
             pltpu.SemaphoreType.DMA((n, 3, 4)),
             pltpu.SemaphoreType.DMA((n, 3, 4)),
             pltpu.SemaphoreType.DMA((n, 4)),
             pltpu.SemaphoreType.DMA((n, 4)),
             pltpu.SemaphoreType.DMA,
+            pltpu.SemaphoreType.DMA((max(1, len(trades)), 3)),
         ],
         compiler_params=pltpu.CompilerParams(collective_id=collective_id, has_side_effects=True),
         name=name,
-    )(piece)
-
-
-def scatter_kernel(dims, parts, n_in, *refs):
-    ins, out_ref, refs = refs[:n_in], refs[n_in], refs[n_in + 1 :]
+    )(piece, *trades)
+
+
+def scatter_kernel(dims, parts, n_in, trades, *refs):
+    ins, refs = refs[:n_in], refs[n_in:]
+    kept, out_ref, given, refs = refs[:trades], refs[trades], refs[trades + 1 : 2 * trades + 1], refs[2 * trades + 1 :]
     n = len(parts)
     work, sib = refs[:n], refs[n : 2 * n]
     bufs = refs[2 * n : 2 * n + 12 * n]
-    load_sem, sib_send, sib_recv, send, recv = refs[14 * n :]
+    load_sem, sib_send, sib_recv, send, recv, trade_sem = refs[14 * n :]
     wdims = tuple(d for d in dims if d != "c")
     me = whereabouts()
     other = moved(me, "c", 1)
@@ -181,9 +215,9 @@
             axis = ORDERS[i][0]
             at = {"x": ALL, "y": ALL, "z": ALL, "c": me["c"], axis: lax.rem(me[axis] + TURN[step] + 4, 4)}
             loads[i, step] = []
-            for j, (k, (c0, width), d0) in enumerate(sources):
+            for j, (k, (c0, width), d0, rows) in enumerate(sources):
                 c = pltpu.make_async_copy(
-                    view(ins[k], dims, at, (c0, width)),
+                    view(ins[k], dims, at, (c0, width), None, rows),
                     view(work[i], wdims, at, (d0, width)),
                     load_sem.at[i, step, j],
                 )
@@ -195,10 +229,10 @@
             axis = ORDERS[i][0]
             at = {"x": ALL, "y": ALL, "z": ALL, "c": other["c"], axis: lax.rem(me[axis] + TURN[step] + 4, 4)}
             pairs[i, step] = []
-            for j, (k, (c0, width), d0) in enumerate(sources):
+            for j, (k, (c0, width), d0, rows) in enumerate(sources):
                 pairs[i, step].append(
                     remote(
-                        view(ins[k], dims, at, (c0, width)),
+                        view(ins[k], dims, at, (c0, width), None, rows),
                         view(sib[i], wdims, at, (d0, width)),
                         sib_send.at[i, step, j],
                         sib_recv.at[i, step, j],
@@ -212,6 +246,7 @@
         sib_sends(step)
         if step:
             own_loads(step)
+    swaps = start_trades(list(zip(kept, given)), trade_sem)
     pending = []
 
     def each_block(at, body):
@@ -319,12 +354,14 @@
     for k in pairs:
         for c in pairs[k]:
             c.wait_send()
-
-
-def scatter(ins, dims, parts, rows, name, collective_id, vmem):
+    for c in swaps:
+        c.wait()
+
+
+def scatter(ins, dims, parts, rows, name, collective_id, vmem, trades=()):
     n = len(parts)
     wdims = tuple(d for d in dims if d != "c")
-    widths = [sum(width for _, (_, width), _ in sources) for sources in parts]
+    widths = [sum(width for _, (_, width), _, _ in sources) for sources in parts]
     wshape = tuple(SIZE[d] for d in wdims)
     dt = ins[0].dtype
     scratch = [pltpu.VMEM(wshape + (rows, w), dt) for w in widths] * 2
@@ -344,19 +381,24 @@
         pltpu.SemaphoreType.DMA((n, 4, most)),
         pltpu.SemaphoreType.DMA((n, 3, 4)),
         pltpu.SemaphoreType.DMA((n, 3, 4)),
+        pltpu.SemaphoreType.DMA((max(1, len(trades)), 3)),
     ]
+    anywhere = pl.BlockSpec(memory_space=pl.ANY)
     lead = (2,) if "l" in dims else ()
     return pl.pallas_call(
-        functools.partial(scatter_kernel, dims, parts, len(ins)),
-        out_shape=jax.ShapeDtypeStruct(lead + (rows, sum(widths)), jnp.float32),
-        in_specs=[pl.BlockSpec(memory_space=pl.ANY)] * len(ins),
-        out_specs=pl.BlockSpec(memory_space=pltpu.VMEM),
+        functools.partial(scatter_kernel, dims, parts, len(ins), len(trades)),
+        out_shape=(
+            jax.ShapeDtypeStruct(lead + (rows, sum(widths)), jnp.float32),
+            *(jax.ShapeDtypeStruct(t.shape, t.dtype) for t in trades),
+        ),
+        in_specs=[anywhere] * (len(ins) + len(trades)),
+        out_specs=(pl.BlockSpec(memory_space=pltpu.VMEM),) + (anywhere,) * len(trades),
         scratch_shapes=scratch,
         compiler_params=pltpu.CompilerParams(
             collective_id=collective_id, has_side_effects=True, vmem_limit_bytes=vmem
         ),
         name=name,
-    )(*ins)
+    )(*ins, *trades)
 
 
 W_DIMS = ("zl", "zh", "x", "y", "c")
@@ -378,6 +420,7 @@
 SIDE = BLOCKS * HALF
 LANES = GROUPS * HALF
 CHUNK = 512
+UNROLL = 2
 VMEM_LIMIT = 56 << 20
 
 
@@ -421,32 +464,50 @@
     return lax.axis_index("ctx") * 2 + lax.axis_index("fsdp")
 
 
-def attend_kernel(kv_ref, q_ref, o_ref, lse_ref, acc_ref):
+def attend_kernel(kv_ref, q_ref, o_ref, lse_ref, *acc_refs):
     me = my_block()
     for side in range(2):
         own = me if side == 0 else BLOCKS - 1 - me
         q = q_ref[0, side]
-        acc_ref[...] = jnp.zeros_like(acc_ref)
-        carry = (jnp.full((1, LANES), NEGATIVE, jnp.float32), jnp.zeros((1, LANES), jnp.float32))
-
-        def step(source, masked, chunk, carry):
-            peak, total = carry
-            kv = kv_ref[source, pl.ds(pl.multiple_of(chunk * CHUNK, CHUNK), CHUNK), :]
-            s = dot_nt(kv, q) * LOG2E
-            if masked:
-                s = jnp.where(seen(source, chunk, side, own), s, NEGATIVE)
-            new = jnp.maximum(peak, jnp.max(s, 0, keepdims=True))
-            p = jnp.exp2(s - new)
-            scale = jnp.exp2(peak - new)
-            total = total * scale + jnp.sum(p, 0, keepdims=True)
-            acc_ref[...] = acc_ref[...] * scale + dot_tn(kv, p.astype(jnp.bfloat16))
-            return new, total
-
+        for acc in acc_refs:
+            acc[...] = jnp.zeros_like(acc)
+        low = jnp.full((1, LANES), NEGATIVE, jnp.float32)
+        none = jnp.zeros((1, LANES), jnp.float32)
+
+        def step(source, masked, width, first, chunk, carry):
+            out = []
+            for u in range(width):
+                peak, total = carry[u]
+                at = first + (chunk - first) * width + u
+                kv = kv_ref[source, pl.ds(pl.multiple_of(at * CHUNK, CHUNK), CHUNK), :]
+                s = dot_nt(kv, q) * LOG2E
+                if masked:
+                    s = jnp.where(seen(source, at, side, own), s, NEGATIVE)
+                new = jnp.maximum(peak, jnp.max(s, 0, keepdims=True))
+                p = jnp.exp2(s - new)
+                scale = jnp.exp2(peak - new)
+                total = total * scale + jnp.sum(p, 0, keepdims=True)
+                acc_refs[u][...] = acc_refs[u][...] * scale + dot_tn(kv, p.astype(jnp.bfloat16))
+                out.append((new, total))
+            return tuple(out) + tuple(carry[width:])
+
+        carry = ((low, none),) * len(acc_refs)
         for source, (edge, whole) in enumerate(chunk_ranges(side, own)):
-            carry = lax.fori_loop(edge[0], edge[1], functools.partial(step, source, True), carry)
-            carry = lax.fori_loop(whole[0], whole[1], functools.partial(step, source, False), carry)
-        peak, total = carry
-        o_ref[0, side] = acc_ref[HEAD_SIZE:, :] / total
+            carry = lax.fori_loop(edge[0], edge[1], functools.partial(step, source, True, 1, edge[0]), carry)
+            start, end = whole
+            for width in (UNROLL, 1):
+                count = lax.div(end - start, width)
+                carry = lax.fori_loop(
+                    start, start + count, functools.partial(step, source, False, width, start), carry
+                )
+                start = start + count * width
+        peak = functools.reduce(jnp.maximum, [c[0] for c in carry])
+        total, out = none, 0.0
+        for (top, part), acc in zip(carry, acc_refs):
+            scale = jnp.exp2(top - peak)
+            total = total + part * scale
+            out = out + acc[HEAD_SIZE:, :] * scale
+        o_ref[0, side] = out / total
         lse_ref[0, side] = peak + jnp.log2(total)
 
 
@@ -466,7 +527,7 @@
             pl.BlockSpec((1, 2, HEAD_SIZE, LANES), lambda h: (h, 0, 0, 0)),
             pl.BlockSpec((1, 2, 1, LANES), lambda h: (h, 0, 0, 0)),
         ),
-        scratch_shapes=[pltpu.VMEM((128, LANES), jnp.float32)],
+        scratch_shapes=[pltpu.VMEM((128, LANES), jnp.float32)] * UNROLL,
         compiler_params=pltpu.CompilerParams(vmem_limit_bytes=VMEM_LIMIT),
         name="attend",
     )(kv, q)
@@ -481,21 +542,29 @@
         lse, delta = lse_ref[0, side], delta_ref[0, side]
         acc_ref[...] = jnp.zeros_like(acc_ref)
 
-        def step(source, masked, chunk, carry):
-            rows = pl.ds(pl.multiple_of(chunk * CHUNK, CHUNK), CHUNK)
-            kv = kv_ref[source, rows, :]
-            p = jnp.exp2(dot_nt(kv, q) * LOG2E - lse)
-            if masked:
-                p = jnp.where(seen(source, chunk, side, own), p, 0.0)
-            ds = (p * (dot_nt(kv, do) - delta)).astype(jnp.bfloat16)
-            more = dot_nn(ds, q) + dot_nn(p.astype(jnp.bfloat16), do)
-            dkv_ref[source, rows, :] = (dkv_ref[source, rows, :].astype(jnp.float32) + more).astype(jnp.bfloat16)
-            acc_ref[...] += dot_tn(kv, ds)
+        def step(source, masked, width, first, chunk, carry):
+            dq = 0.0
+            for u in range(width):
+                at = first + (chunk - first) * width + u
+                rows = pl.ds(pl.multiple_of(at * CHUNK, CHUNK), CHUNK)
+                kv = kv_ref[source, rows, :]
+                p = jnp.exp2(dot_nt(kv, q) * LOG2E - lse)
+                if masked:
+                    p = jnp.where(seen(source, at, side, own), p, 0.0)
+                ds = (p * (dot_nt(kv, do) - delta)).astype(jnp.bfloat16)
+                more = dot_nn(ds, q) + dot_nn(p.astype(jnp.bfloat16), do)
+                dkv_ref[source, rows, :] = (dkv_ref[source, rows, :].astype(jnp.float32) + more).astype(jnp.bfloat16)
+                dq = dq + dot_tn(kv, ds)
+            acc_ref[...] += dq
             return carry
 
         for source, (edge, whole) in enumerate(chunk_ranges(side, own)):
-            lax.fori_loop(edge[0], edge[1], functools.partial(step, source, True), 0)
-            lax.fori_loop(whole[0], whole[1], functools.partial(step, source, False), 0)
+            lax.fori_loop(edge[0], edge[1], functools.partial(step, source, True, 1, edge[0]), 0)
+            start, end = whole
+            for width in (UNROLL, 1):
+                count = lax.div(end - start, width)
+                lax.fori_loop(start, start + count, functools.partial(step, source, False, width, start), 0)
+                start = start + count * width
         dq_ref[0, side] = acc_ref[:HEAD_SIZE, :]
 
 
@@ -550,6 +619,162 @@
     return jnp.transpose(h, (1, 4, 0, 3, 2)).reshape(2 * HALF, QH * HEAD_SIZE)
 
 
+def outer_kernel(left_ref, right_ref, out_ref):
+    out_ref[0] = dot_tn(left_ref[...], right_ref[0]).astype(jnp.bfloat16)
+
+
+def outer(left, right, steps):
+    tokens, m = left.shape
+    n = right.shape[-1]
+    return pl.pallas_call(
+        outer_kernel,
+        grid=(2, steps),
+        out_shape=jax.ShapeDtypeStruct((2, m, n), jnp.bfloat16),
+        in_specs=[
+            pl.BlockSpec((tokens, m // steps), lambda h, s: (0, s)),
+            pl.BlockSpec((1, tokens, n), lambda h, s: (h, 0, 0)),
+        ],
+        out_specs=pl.BlockSpec((1, m // steps, n), lambda h, s: (h, s, 0)),
+        compiler_params=pltpu.CompilerParams(vmem_limit_bytes=VMEM_LIMIT),
+        name="outer",
+    )(left, right)
+
+
+def thirds(rows):
+    high = rows.astype(jnp.bfloat16)
+    rest = rows - high.astype(jnp.float32)
+    middle = rest.astype(jnp.bfloat16)
+    return high, middle, (rest - middle.astype(jnp.float32)).astype(jnp.bfloat16)
+
+
+def ffn_kernel(
+    whole_ref, attn_ref, x_ref, dy_ref, gain_ref, spread_ref, spread_down_ref,
+    layer_out_ref, middle_grad_ref, attn_grad_ref, attn_wide_ref, normed_ref, gate_low_ref, up_low_ref,
+    inner_ref, middle_low_ref, gain_grad_ref,
+    w_out, w_gate, w_up, w_down, gate_s, up_s, sems,
+):
+    bf, f32 = jnp.bfloat16, jnp.float32
+
+    def fetch(dst, start, width, sem):
+        c = pltpu.make_async_copy(whole_ref.at[:, :, :, pl.ds(start, width)], dst, sem)
+        c.start()
+        return c
+
+    get_out = fetch(w_out, 3584, 512, sems.at[0])
+    get_gate = fetch(w_gate, 0, 1280, sems.at[1])
+    get_up = fetch(w_up, 1792, 1280, sems.at[2])
+    get_down = [
+        fetch(w_down.at[:, :, pl.ds(16 * g, 16), :], 1280 + 1792 * g, 512, sems.at[3 + g]) for g in range(3)
+    ]
+    real = lax.broadcasted_iota(jnp.int32, (128, 512), 1) < 480
+
+    attn_wide = 0.0
+    for h in range(2):
+        attn_wide = attn_wide + dot_nn(attn_ref[h].astype(bf), spread_ref[h])
+    attn_wide = attn_wide.astype(bf)
+    attn_wide_ref[...] = attn_wide
+    get_out.wait()
+    middle, squares = [], 0.0
+    for h in range(2):
+        part = dot_nn(attn_wide, w_out[h].reshape(1024, 512))
+        part = x_ref[h].astype(f32) + jnp.where(real, part, 0.0)
+        squares = squares + jnp.sum(part * part, -1, keepdims=True)
+        middle.append(part)
+    factor = lax.rsqrt(squares / 960 + EPS)
+    normed = 0.0
+    for h in range(2):
+        normed = normed + dot_nn((middle[h] * factor * gain_ref[h]).astype(bf), spread_ref[h])
+    normed = normed.astype(bf)
+    normed_ref[...] = normed
+    get_gate.wait()
+    get_up.wait()
+    for h in range(2):
+        gate = dot_nn(normed, w_gate[h].reshape(1024, 1280))
+        up = dot_nn(normed, w_up[h].reshape(1024, 1280))
+        gate_s[h], up_s[h] = gate, up
+        inner = (gate * jax.nn.sigmoid(gate) * up).astype(bf)
+        for b in range(2):
+            inner_ref[:, pl.ds(768 * (2 * h + b), 768)] = dot_nn(
+                inner[:, 640 * b : 640 * b + 640], spread_down_ref[...]
+            ).astype(bf)
+    for c in get_down:
+        c.wait()
+    for h in range(2):
+        low = dot_nn(inner_ref[...], w_down[h].reshape(3072, 512))
+        layer_out_ref[h] = (middle[h] + low).astype(bf)
+    normed_grad = 0.0
+    for h in range(2):
+        for b in range(2):
+            blocks = pl.ds(16 * (2 * h + b), 16)
+            wide_grad = 0.0
+            for d in range(2):
+                wide_grad = wide_grad + dot_nt(dy_ref[d], w_down[d, blocks].reshape(768, 512))
+            inner_grad = 0.0
+            for t in thirds(wide_grad):
+                inner_grad = inner_grad + dot_nt(t, spread_down_ref[...])
+            cols = pl.ds(640 * b, 640)
+            gate, up = gate_s[h, :, cols], up_s[h, :, cols]
+            sigma = jax.nn.sigmoid(gate)
+            gate_low_ref[h, :, cols] = (inner_grad * up * sigma * (1.0 + gate * (1.0 - sigma))).astype(bf)
+            up_low_ref[h, :, cols] = (inner_grad * (gate * sigma)).astype(bf)
+        normed_grad = normed_grad + dot_nt(gate_low_ref[h], w_gate[h].reshape(1024, 1280))
+        normed_grad = normed_grad + dot_nt(up_low_ref[h], w_up[h].reshape(1024, 1280))
+    split = thirds(normed_grad)
+    grads, mean = [], 0.0
+    for h in range(2):
+        g = 0.0
+        for t in split:
+            g = g + dot_nt(t, spread_ref[h])
+        gain_grad_ref[h] = jnp.sum(g * middle[h] * factor, 0, keepdims=True)
+        g = g * gain_ref[h]
+        mean = mean + jnp.sum(g * middle[h], -1, keepdims=True)
+        grads.append(g)
+    wide_grad = 0.0
+    for h in range(2):
+        total = dy_ref[h].astype(f32) + factor * grads[h] - middle[h] * (factor * factor * factor * (mean / 960))
+        middle_grad_ref[h] = total
+        middle_low_ref[h] = total.astype(bf)
+        wide_grad = wide_grad + dot_nt(total.astype(bf), w_out[h].reshape(1024, 512))
+    wide_grad = wide_grad.astype(bf)
+    for h in range(2):
+        attn_grad_ref[h] = dot_nt(wide_grad, spread_ref[h]).astype(bf)
+
+
+def ffn(whole, attn, x, dy, gain, spread, spread_down):
+    bf, f32 = jnp.bfloat16, jnp.float32
+    vmem = pl.BlockSpec(memory_space=pltpu.VMEM)
+    shapes = [
+        ((2, 128, 512), bf), ((2, 128, 512), f32), ((2, 128, 512), bf), ((128, 1024), bf), ((128, 1024), bf),
+        ((2, 128, 1280), bf), ((2, 128, 1280), bf), ((128, 3072), bf), ((2, 128, 512), bf), ((2, 1, 512), f32),
+    ]
+    return pl.pallas_call(
+        ffn_kernel,
+        out_shape=tuple(jax.ShapeDtypeStruct(s, d) for s, d in shapes),
+        in_specs=[pl.BlockSpec(memory_space=pl.ANY)] + [vmem] * 6,
+        out_specs=(vmem,) * len(shapes),
+        scratch_shapes=[
+            pltpu.VMEM((2, 64, 16, 512), bf),
+            pltpu.VMEM((2, 64, 16, 1280), bf),
+            pltpu.VMEM((2, 64, 16, 1280), bf),
+            pltpu.VMEM((2, 64, 48, 512), bf),
+            pltpu.VMEM((2, 128, 1280), f32),
+            pltpu.VMEM((2, 128, 1280), f32),
+            pltpu.SemaphoreType.DMA((6,)),
+        ],
+        compiler_params=pltpu.CompilerParams(vmem_limit_bytes=VMEM_LIMIT),
+        name="ffn",
+    )(whole, attn, x, dy, gain, spread, spread_down)
+
+
+def halves(rows):
+    both = jnp.stack([rows[:, :480], rows[:, 480:]])
+    return jnp.pad(both, ((0, 0), (0, 0), (0, 32)))
+
+
+def joined(both):
+    return jnp.concatenate([both[0, :, :480], both[1, :, :480]], 1)
+
+
 def local(
     layer_in,
     attn_gain,
@@ -565,53 +790,34 @@
 ):
     bf, f32 = jnp.bfloat16, jnp.float32
     me = my_block()
-    swap = [(i, BLOCKS - 1 - i) for i in range(BLOCKS)]
-
-    def exchanged(rows):
-        return lax.ppermute(rows, ("ctx", "fsdp"), swap)
-
-    both = jnp.concatenate([layer_in, out_cotangent], 1)
-    both = jnp.concatenate([both[:HALF], exchanged(both[HALF:])], 0)
-    x_low, dy = both[:, :960], both[:, 960:]
 
     down = jnp.zeros((48, 512), bf)
     down = down.at[:40, :480].set(down_weight)
     down = down.at[40, :15].set(attn_gain).at[41, :15].set(ffn_gain)
     down = down.reshape(3, 16, 512)
-    qkvo = jnp.concatenate([query_weight, key_weight, value_weight, output_weight], 1)
-    mats = [jnp.pad(a, ((0, 1), (0, 0))) for a in (gate_weight, up_weight, qkvo)]
+    oqkv = jnp.concatenate([output_weight, query_weight, key_weight, value_weight], 1)
+    mats = [jnp.pad(a, ((0, 1), (0, 0))) for a in (gate_weight, up_weight, oqkv)]
     piece = jnp.concatenate([a for i in range(3) for a in (mats[i], down[i])], 1)
-    whole = gather(piece, W_DIMS, W_PARTS, "gather_weights", 1).reshape(2, 64, 16, 5376)
-    flat = whole.reshape(2, 1024, 5376)
-    w_gate, w_up = flat[:, :, :1280], flat[:, :, 1792:3072]
-    w_qkv, w_out = flat[:, :, 3584:4384], flat[:, :, 4384:4864]
-    w_down = jnp.stack([whole[..., 1280:1792], whole[..., 3072:3584], whole[..., 4864:5376]], 2)
-    w_down = w_down.reshape(2, 64, 48, 512)[:, :, :40, :480].reshape(2, 2560, 480)
+    whole, x_low, dy = gather(piece, W_DIMS, W_PARTS, "gather_weights", 1, (layer_in, out_cotangent))
+    whole = whole.reshape(2, 64, 16, 5376)
+    w_qkv = whole.reshape(2, 1024, 5376)[:, :, 4064:4864]
     gain_one = whole[0, :, 8, 4864:4880].reshape(1024).astype(f32)
-    gain_two = whole[0, :, 9, 4864:4879].reshape(960).astype(f32)
-
-    i = lax.broadcasted_iota(jnp.int32, (960, 1024), 0)
-    j = lax.broadcasted_iota(jnp.int32, (960, 1024), 1)
-    spread = (j == (i // 15) * 16 + i % 15).astype(bf)
-
-    def wide(rows):
-        return mm("td,de->te", rows, spread)
-
-    def narrow_low(rows):
-        return mm("te,de->td", rows, spread)
-
-    def narrow(rows):
-        high = rows.astype(bf)
-        rest = rows - high.astype(f32)
-        middle = rest.astype(bf)
-        last = (rest - middle.astype(f32)).astype(bf)
-        return narrow_low(high) + narrow_low(middle) + narrow_low(last)
+    gain_two = whole[0, :, 9, 4864:4879].reshape(1, 960).astype(f32)
+
+    i = lax.broadcasted_iota(jnp.int32, (2, 512, 1024), 1)
+    d = i + 480 * lax.broadcasted_iota(jnp.int32, (2, 512, 1024), 0)
+    j = lax.broadcasted_iota(jnp.int32, (2, 512, 1024), 2)
+    spread = jnp.logical_and(i < 480, j == (d // 15) * 16 + d % 15).astype(bf)
+    i = lax.broadcasted_iota(jnp.int32, (640, 768), 0)
+    j = lax.broadcasted_iota(jnp.int32, (640, 768), 1)
+    spread_down = (j == (i // 40) * 48 + i % 40).astype(bf)
 
     t = jnp.arange(HALF, dtype=jnp.int32)
     positions = jnp.concatenate([me * 128 + t, (BLOCKS - 1 - me) * 128 + HALF + t])
     cosine, sine = rotary_tables(positions)
 
-    hidden = wide(x_low)
+    x_halves, dy_halves = halves(x_low), halves(dy)
+    hidden = mm("htd,hde->te", x_halves, spread)
     factor_one = lax.rsqrt(jnp.sum(hidden * hidden, -1, keepdims=True) / 960 + EPS)
     normed = (hidden * factor_one * gain_one).astype(bf)
     qkv = mm("te,hec->thc", normed, w_qkv)
@@ -623,47 +829,22 @@
     kv_piece = jnp.concatenate(
         [key_rot.reshape(2, HALF, KEY_HEADS, 64), value.astype(bf).reshape(2, HALF, KEY_HEADS, 64)], -1
     ).reshape(2, HALF, 640)
-    kv = gather(kv_piece, T_DIMS, T_PARTS, "gather_keys", 2).reshape(2, SIDE, 640)
+    (kv,) = gather(kv_piece, T_DIMS, T_PARTS, "gather_keys", 2)
+    kv = kv.reshape(2, SIDE, 640)
     q_heads = jnp.pad(by_head(query_rot * jnp.asarray(0.125, bf)), ((0, 0), (0, 0), (0, 0), (0, 64)))
     attn_heads, lse = attend(kv, q_heads)
     attn = by_token(attn_heads)
-    attn_low = attn.astype(bf)
-    attn_wide = wide(attn_low).astype(bf)
-    middle = x_low.astype(f32) + mm("te,hec->thc", attn_wide, w_out).reshape(128, 960)
-    factor_two = lax.rsqrt(jnp.mean(middle * middle, -1, keepdims=True) + EPS)
-    normed_two = wide((middle * factor_two * gain_two).astype(bf)).astype(bf)
-    gate = mm("te,hec->thc", normed_two, w_gate)
-    upward = mm("te,hec->thc", normed_two, w_up)
-    sigma = jax.nn.sigmoid(gate)
-    activated = gate * sigma
-    inner = (activated * upward).astype(bf)
-    inner_flat = inner.reshape(128, 2560)
-    layer_out = (middle + mm("tf,hfd->thd", inner_flat, w_down).reshape(128, 960)).astype(bf)
-    layer_out = jnp.concatenate([layer_out[:HALF], exchanged(layer_out[HALF:])], 0)
-
-    dy_split = dy.reshape(128, 2, 480)
-    inner_grad = mm("thd,hfd->tf", dy_split, w_down).reshape(128, 2, 1280)
-    gate_low = (inner_grad * upward * sigma * (1.0 + gate * (1.0 - sigma))).astype(bf)
-    up_low = (inner_grad * activated).astype(bf)
-    down_term = mm("tf,thd->hfd", inner_flat, dy_split).astype(bf)
-    gate_term = mm("te,thc->hec", normed_two, gate_low).astype(bf)
-    up_term = mm("te,thc->hec", normed_two, up_low).astype(bf)
-    grad_two = narrow(mm("thc,hec->te", gate_low, w_gate) + mm("thc,hec->te", up_low, w_up))
-    weighted = gain_two * grad_two
-    middle_grad = dy.astype(f32) + (
-        factor_two * weighted - middle * factor_two**3 * jnp.mean(weighted * middle, -1, keepdims=True)
+    (layer_out, middle_grad, attn_grad, attn_wide, normed_two, gate_low, up_low, inner, middle_low, gain_two_term) = ffn(
+        whole, halves(attn), x_halves, dy_halves, halves(gain_two), spread, spread_down
     )
-    gain_two_term = jnp.sum(grad_two * middle * factor_two, 0)
-    middle_low = middle_grad.astype(bf)
-    out_term = mm("te,thd->hed", attn_wide, middle_low.reshape(128, 2, 480)).astype(bf)
-    attn_grad = narrow_low(mm("thd,hed->te", middle_low.reshape(128, 2, 480), w_out).astype(bf)).astype(bf)
+    layer_out, middle_grad, attn_grad = joined(layer_out), joined(middle_grad), joined(attn_grad)
     delta = jnp.sum((attn_grad.astype(f32) * attn).reshape(2, HALF, KEY_HEADS, GROUPS, HEAD_SIZE), -1)
     delta = jnp.transpose(delta, (2, 0, 3, 1)).reshape(KEY_HEADS, 2, 1, LANES)
     do_heads = jnp.pad(by_head(attn_grad), ((0, 0), (0, 0), (0, 0), (64, 0)))
     dq_heads, dkv = attend_back(kv, q_heads, do_heads, lse, delta)
     dkv = dkv.reshape(2, 2, 4, 4, 2, 2, HALF, 640)
-    parts = tuple(((0, c, 0),) for c in T_PARTS)
-    key_sums = scatter([dkv], T_DIMS, parts, HALF, "scatter_keys", 3, VMEM_LIMIT)
+    parts = tuple(((0, c, 0, ALL),) for c in T_PARTS)
+    key_sums, layer_out = scatter([dkv], T_DIMS, parts, HALF, "scatter_keys", 3, VMEM_LIMIT, (layer_out,))
     key_sums = key_sums.reshape(128, KEY_HEADS, 128)
     query_low = rotate(by_token(dq_heads) * 0.125, cosine, -sine).astype(bf)
     key_low = rotate(key_sums[..., :64].reshape(128, 320), cosine, -sine).astype(bf)
@@ -671,38 +852,43 @@
     qkv_low = jnp.concatenate(
         [query_low.reshape(128, 2, 480), key_low.reshape(128, 2, 160), value_low.reshape(128, 2, 160)], -1
     )
-    qkv_term = mm("te,thc->hec", normed, qkv_low).astype(bf)
     normed_grad = mm("thc,hec->te", qkv_low, w_qkv)
     weighted = gain_one * normed_grad
     input_back = factor_one * weighted - hidden * factor_one**3 * (
         jnp.sum(weighted * hidden, -1, keepdims=True) / 960
     )
     gain_one_term = jnp.sum(normed_grad * hidden * factor_one, 0)
-    input_grad = middle_grad + narrow(input_back)
-    input_grad = jnp.concatenate([input_grad[:HALF], exchanged(input_grad[HALF:])], 0)
-
-    qkvo_term = jnp.concatenate([qkv_term, out_term], -1)
-    down_pad = jnp.pad(down_term.reshape(2, 64, 40, 480), ((0, 0), (0, 0), (0, 0), (0, 32)))
-    gains = jnp.stack(
-        [gain_one_term.reshape(64, 16)[:, :15], gain_two_term.reshape(64, 15)], 1
-    ).astype(bf)
-    gains = jnp.pad(gains, ((0, 0), (0, 6), (0, 512 - 15)))
-    down_pad = jnp.concatenate([down_pad, jnp.broadcast_to(gains, (2, 64, 8, 512))], 2)
-    down_pad = jnp.transpose(down_pad.reshape(2, 64, 3, 16, 512), (0, 1, 3, 2, 4)).reshape(2, 64, 16, 1536)
-    terms = [gate_term, up_term, qkvo_term, down_pad]
-    terms = [lax.optimization_barrier(a).reshape(2, 2, 4, 4, 2, 16, -1) for a in terms]
-    parts = tuple(((k, (0, 1280), 0), (3, (512 * k, 512), 1280)) for k in range(3))
-    sums = scatter(terms, W_DIMS, parts, 16, "scatter_weights", 4, VMEM_LIMIT)
+    input_back = sum(mm("te,hde->htd", part, spread) for part in thirds(input_back))
+    input_grad = middle_grad + joined(input_back)
+
+    gains = jnp.concatenate([gain_one_term.reshape(64, 16)[:, :15], joined(gain_two_term).reshape(64, 15)], 1)
+    gains = jnp.pad(gains.astype(bf), ((0, 0), (0, 1280 - 30)))
+    right = jnp.concatenate(
+        [
+            jnp.pad(jnp.transpose(qkv_low, (1, 0, 2)), ((0, 0), (0, 0), (480, 0))),
+            jnp.pad(middle_low[:, :, :480], ((0, 0), (0, 0), (0, 800))),
+            jnp.stack([gains, gains]),
+        ],
+        1,
+    )
+    slot = lax.broadcasted_iota(jnp.int32, (64, 1024), 0) * 16 + 15
+    slot = (slot == lax.broadcasted_iota(jnp.int32, (64, 1024), 1)).astype(bf)
+    left = jnp.concatenate([normed, attn_wide, slot], 0)
+    terms = [outer(normed_two, gate_low, 2), outer(normed_two, up_low, 2), outer(left, right, 2)]
+    terms = [a.reshape(2, 2, 4, 4, 2, 16, 1280) for a in terms]
+    terms.append(outer(inner, dy_halves, 3).reshape(2, 2, 4, 4, 2, 48, 512))
+    parts = tuple(((k, (0, 1280), 0, ALL), (3, (0, 512), 1280, pl.ds(16 * k, 16))) for k in range(3))
+    sums, input_grad = scatter(terms, W_DIMS, parts, 16, "scatter_weights", 4, VMEM_LIMIT, (input_grad,))
     down_sum = jnp.concatenate([sums[:, 1280:1792], sums[:, 3072:3584], sums[:, 4864:5376]], 0)
     return (
         layer_out,
         input_grad,
-        down_sum[40, :15],
+        sums[15, 3584:3599],
+        sums[:15, 4064:4544],
+        sums[:15, 4544:4704],
+        sums[:15, 4704:4864],
         sums[:15, 3584:4064],
-        sums[:15, 4064:4224],
-        sums[:15, 4224:4384],
-        sums[:15, 4384:4864],
-        down_sum[41, :15],
+        sums[15, 3599:3614],
         sums[:15, :1280],
         sums[:15, 1792:3072],
         down_sum[:40, :480],

time: 694 us -> 611 us (0.88)
  local copies, waits for them, and re-layouts: 91.2 us -> 38.6 us
  matrix products: 63.9 us -> 16.5 us
  Pallas kernels: 480 us -> 523 us
  starting transfers between devices: 15.8 us -> 0 us
    pallas_call x4 -> x9, Pallas kernels: 278 us -> 350 us  [the longest x2 153 us: scatter(): pl.pallas_call(functools.partial(scatter_kernel, dims, parts, len(ins), l...]
    dot_general x24 -> x6, matrix products: 63.9 us -> 16.5 us  [mm(): return jnp.einsum(form, left, right, preferred_element_type=jnp.float32)]
    optimization_barrier x3 -> x0, local copies, waits for them, and re-layouts: 23.9 us -> none  [local(): lax.optimization_barrier(a).reshape(2, 2, 4, 4, 2, 16, -1)]
    pallas_call x1, Pallas kernels: 106 us -> 84.4 us  [attend_back(): pl.pallas_call(attend_back_kernel, grid=(KEY_HEADS,), out_shape=(jax.Shap...]
    ppermute x3 -> x0, starting transfers between devices: 15.8 us -> none  [exchanged(): return lax.ppermute(rows, ('ctx', 'fsdp'), swap)]
    reshape x3 -> x1, local copies, waits for them, and re-layouts: 11.8 us -> 0.15 us  [local(): joined(gain_two_term).reshape(64, 15)]
    convert_element_type x3 -> x4, local copies, waits for them, and re-layouts: 10.2 us -> 0.52 us  [the longest x1 0.14 us: local(): query_low = rotate(by_token(dq_heads) * 0.125, cosine, -sine).astype(bf)]
    pallas_call x1, Pallas kernels: 95.8 us -> 88.8 us  [attend(): pl.pallas_call(attend_kernel, grid=(KEY_HEADS,), out_shape=(jax.ShapeDtyp...]
  transfers between devices with their start and end apart: 3 -> 0, of which waited for: 1 -> 0; matrix products, arithmetic and copies ran while one was open for 6% -> 0% of each run, Pallas kernels for 9% -> 0%
where the time goes in v2:
time: 611 us; the launch traced here: 602 us
  Pallas kernels  523 us (86%)
  local copies, waits for them, and re-layouts  38.6 us (6%)
  other arithmetic  22.2 us (4%)
  matrix products  16.5 us (3%)
    pallas_call x2, Pallas kernels, scatter(): pl.pallas_call(functools.partial(scatter_kernel, dims, parts, len(ins), l...  153 us
    pallas_call x2, Pallas kernels, gather(): pl.pallas_call(functools.partial(gather_kernel, dims, parts, len(trades))...  150 us
    pallas_call x1, Pallas kernels, attend(): pl.pallas_call(attend_kernel, grid=(KEY_HEADS,), out_shape=(jax.ShapeDtyp...  88.8 us
    pallas_call x1, Pallas kernels, attend_back(): pl.pallas_call(attend_back_kernel, grid=(KEY_HEADS,), out_shape=(jax.Shap...  84.4 us
    pallas_call x4, Pallas kernels, outer(): pl.pallas_call(outer_kernel, grid=(2, steps), out_shape=jax.ShapeDtypeStr...  23.9 us
    pallas_call x1, Pallas kernels, ffn(): pl.pallas_call(ffn_kernel, out_shape=tuple((jax.ShapeDtypeStruct(s, d) fo...  22.8 us
    dot_general x6, matrix products, mm(): return jnp.einsum(form, left, right, preferred_element_type=jnp.float32)  16.5 us

profile of v2, /device:TPU:0, one launch (start us, length us, event | category | flops | bytes accessed | tf_op | source)
XLA Modules:
  0.0 601.9 jit_solution(8045609926439557547)
XLA Ops:
  4.6 0.8 concatenate.70
  5.5 1.9 copy.70.refs_1_
  7.3 1.8 copy.71.refs_2_
  9.1 78.8 %gather_weights.1 = (bf16[2,2,4,4,2,16,5376]{6,5,4,3,2,1,0:T(8,128)(2,1)}, bf16[128,960]{1,0:T(8,128)(2,1)}, bf16[128,960]{1,0:T(8,128)(2,1)}) custom-call(bf16[16,5376]{1,0:T(8,128)(2,1)} %copy-done.5, bf16[128,960]{1,0:T(8,128)(2,1)} %copy.70.refs_1_, bf16[128,960]{1,0:T(8,128)(2,1)} %copy.71.refs_2_), custom_call_target="tpu_custom_call" | custom-call | tf_op jit(solution)/shard_map/gather_weights/pallas_call | solution.py:168
  87.9 1.9 slice_bitcast_fusion.11
  89.9 1.8 multiply_reduce_fusion.3
  92.2 1.0 fusion.48
  94.2 5.5 fusion.12
  100.9 1.1 copy.81
  102.0 0.9 pad.61.q_ref
  104.9 0.9 reshape.339.refs_0_
  105.8 71.1 %gather_keys.1 = bf16[2,2,4,4,2,2,64,640]{7,6,5,4,3,2,1,0:T(8,128)(2,1)} custom-call(bf16[2,64,640]{2,1,0:T(8,128)(2,1)} %reshape.339.refs_0_), custom_call_target="tpu_custom_call" | custom-call | tf_op jit(solution)/shard_map/gather_keys/pallas_call | solution.py:168
  176.9 88.8 %attend.1 = (f32[5,2,64,192]{3,2,1,0:T(8,128)}, f32[5,2,1,192]{3,2,1,0:T(1,128)}) custom-call(bf16[2,8192,640]{2,1,0:T(8,128)(2,1)} %bitcast.99, bf16[5,2,192,128]{3,2,1,0:T(8,128)(2,1)} %pad.61.q_ref), custom_call_target="tpu_custom_call" | custom-call | tf_op jit(solution)/shard_map/attend/pallas_call | solution.py:515
  265.7 1.4 copy.82
  268.6 0.8 select_maximum_fusion.attn_ref
  269.4 1.7 fusion.40.x_ref
  271.1 1.6 fusion.41.dy_ref.right_ref
  272.8 1.0 fusion.47
  274.6 3.5 fusion.27.spread_ref
  278.1 2.4 fusion.16.spread_down_ref
  280.6 22.8 %ffn.1 = (bf16[2,128,512]{2,1,0:T(8,128)(2,1)}, f32[2,128,512]{2,1,0:T(8,128)}, bf16[2,128,512]{2,1,0:T(8,128)(2,1)}, bf16[128,1024]{1,0:T(8,128)(2,1)}, bf16[12...) custom-call(bf16[2,64,16,5376]{3,2,1,0:T(8,128)(2,1)} %bitcast.105, ...), custom_call_target="tpu_custom_call" | custom-call | tf_op jit(solution)/shard_map/ffn/pallas_call | solution.py:750
  303.4 1.0 slice_bitcast_fusion.9
  304.9 1.3 copy.88
  307.2 1.1 copy.87
  308.3 1.0 pad.65.do_ref
  309.3 84.4 %attend_back.1 = (f32[5,2,64,192]{3,2,1,0:T(8,128)}, bf16[2,8192,640]{2,1,0:T(8,128)(2,1)}) custom-call(bf16[2,8192,640]{2,1,0:T(8,128)(2,1)} %bitcast.100, bf16[5,2,192,128]{3,2,1,0:T(8,128)(2,1)} %pad.61.q_ref, bf16[5,2,192,128]{3,2,1,0:T(8,128)(2,1)} %pad.65.do_ref, f32[5,2,1,192]{3,2,1,0:T(1,128)} %get-tuple-element.73.lse_ref, ...), custom_call_target="tpu_custom_call" | custom-call | tf_op jit(solution)/shard_map/attend_back/pallas_call | solution.py:575
  393.7 1.2 broadcast_multiply_fusion
  395.2 1.2 copy.91
  398.2 84.3 %scatter_keys.1 = (f32[2,64,640]{2,1,0:T(8,128)}, bf16[128,960]{1,0:T(8,128)(2,1)}) custom-call(bf16[2,2,4,4,2,2,64,640]{7,6,5,4,3,2,1,0:T(8,128)(2,1)} %bitcast.108, bf16[128,960]{1,0:T(8,128)(2,1)} %pad_maximum_fusion.4.refs_1_), custom_call_target="tpu_custom_call" | custom-call | tf_op jit(solution)/shard_map/scatter_keys/pallas_call | solution.py:388
  482.5 1.0 reshape.350
  484.9 3.9 multiply_reduce_fusion.1
  489.1 1.8 fusion.25
  490.8 1.8 convolution_add_fusion.1
  492.6 1.8 fusion.19
  494.5 1.1 maximum_add_fusion.refs_4_
  495.6 6.7 %outer.7 = bf16[2,3072,512]{2,1,0:T(8,128)(2,1)} custom-call(bf16[128,3072]{1,0:T(8,128)(2,1)} %get-tuple-element.85.left_ref, bf16[2,128,512]{2,1,0:T(8,128)(2,1)} %fusion.41.dy_ref.right_ref), custom_call_target="tpu_custom_call" | custom-call | tf_op jit(solution)/shard_map/outer/pallas_call | solution.py:629
  502.9 1.5 fusion.18.right_ref
  504.5 0.9 pad_maximum_fusion.left_ref
  505.4 6.7 %outer.6 = bf16[2,1024,1280]{2,1,0:T(8,128)(2,1)} custom-call(bf16[320,1024]{1,0:T(8,128)(2,1)} %pad_maximum_fusion.left_ref, bf16[2,320,1280]{2,1,0:T(8,128)(2,1)} %fusion.18.right_ref), custom_call_target="tpu_custom_call" | custom-call | tf_op jit(solution)/shard_map/outer/pallas_call | solution.py:629
  512.1 5.2 outer.5
  517.3 5.2 outer.4
  522.5 68.7 %scatter_weights.1 = (f32[16,5376]{1,0:T(8,128)}, f32[128,960]{1,0:T(8,128)}) custom-call(bf16[2,2,4,4,2,16,1280]{6,5,4,3,2,1,0:T(8,128)(2,1)} %bitcast.110, bf16[2,2,4,4,2,16,1280]{6,5,4,3,2,1,0:T(8,128)(2,1)} %bitcast.109, bf16[2,2,4,4,2,16,1280]{6,5,4,3,2,1,0:T(8,128)(2,1)} %bitcast.107, bf16[2,2,4,4,2,48,512]{6,5,4,3,2,1,0:T(8,128)(2,1)} %bitcast.101, ...), custom_call_target="tpu_custom_call" | custom-call | tf_op jit(solution)/shard_map/scatter_weights/pallas_call | solution.py:388
  592.7 2.0 copy.104
  594.7 1.6 fusion.80
  596.3 1.5 fusion.81
  597.9 1.5 fusion.82
  599.4 1.3 slice_bitcast_fusion.18
  600.7 0.8 copy.103
  (124 shorter events, 17.9 us)
Async XLA Ops:
  5.5 3.7 copy-start.5
  89.8 1.9 copy-start.3
  89.8 1.9 copy-start.4
  89.8 1.9 copy-start.17
  89.9 1.9 copy-start.19
  92.2 8.7 %copy-start.14 = (f32[128]{0:T(128)}, f32[128]{0:T(128)S(1)}, u32[]{:S(2)}) copy-start(f32[128]{0:T(128)S(1)} %get-tuple-element.167) | copy-start | bytes 1540
  93.3 7.6 %copy-start.11 = (f32[1024]{0:T(1024)}, f32[1024]{0:T(1024)S(1)}, u32[]{:S(2)}) copy-start(f32[1024]{0:T(1024)S(1)} %reshape.355) | copy-start | bytes 12292
  93.4 0.7 copy-start
  393.7 3.3 copy-start.10
  393.7 3.6 copy-start.9
  482.5 2.4 copy-start.12
  482.5 2.4 copy-start.15
  484.3 4.6 copy-start.16
  484.9 4.1 copy-start.18
  484.9 4.1 copy-start.20
  492.6 1.8 copy-start.2
  494.5 7.9 %copy-start.13 = (f32[2,1,512]{2,1,0:T(1,128)S(1)}, f32[2,1,512]{2,1,0:T(1,128)}, u32[]{:S(2)}) copy-start(f32[2,1,512]{2,1,0:T(1,128)} %get-tuple-element.84) | copy-start | bytes 12292
  495.6 7.3 %copy-start.7 = (bf16[2,128,512]{2,1,0:T(8,128)(2,1)S(1)}, bf16[2,128,512]{2,1,0:T(8,128)(2,1)}, u32[]{:S(2)}) copy-start(bf16[2,128,512]{2,1,0:T(8,128)(2,1)} %get-tuple-element.83) | copy-start | bytes 786436
  495.6 8.9 %copy-start.1 = (bf16[128,1024]{1,0:T(8,128)(2,1)S(1)}, bf16[128,1024]{1,0:T(8,128)(2,1)}, u32[]{:S(2)}) copy-start(bf16[128,1024]{1,0:T(8,128)(2,1)} %copy-done) | copy-start | bytes 786436
  495.6 8.9 %copy-start.6 = (bf16[128,1024]{1,0:T(8,128)(2,1)S(1)}, bf16[128,1024]{1,0:T(8,128)(2,1)}, u32[]{:S(2)}) copy-start(bf16[128,1024]{1,0:T(8,128)(2,1)} %get-tuple-element.80) | copy-start | bytes 786436
  522.5 78.2 %copy-start.8 = (bf16[128,960]{1,0:T(8,128)(2,1)S(1)}, bf16[128,960]{1,0:T(8,128)(2,1)}, u32[]{:S(2)}) copy-start(bf16[128,960]{1,0:T(8,128)(2,1)} %get-tuple-element.111) | copy-start | bytes 737284

commit v3 on v2

--- a/solution.py
+++ b/solution.py
@@ -419,32 +419,33 @@
 HALF = 64
 SIDE = BLOCKS * HALF
 LANES = GROUPS * HALF
-CHUNK = 512
+CHUNK = 2048
+BACK_CHUNK = 1024
 UNROLL = 2
 VMEM_LIMIT = 56 << 20
 
 
-def chunk_ranges(side, own):
-    count = SIDE // CHUNK
+def chunk_ranges(side, own, size):
+    count = SIDE // size
     if side == 0:
-        diag = lax.div(HALF * own, CHUNK)
+        diag = lax.div(HALF * own, size)
         first = HALF * (BLOCKS - own)
-        edge, whole = lax.div(first, CHUNK), lax.div(first + CHUNK - 1, CHUNK)
+        edge, whole = lax.div(first, size), lax.div(first + size - 1, size)
         return ((diag, diag + 1), (0, diag)), ((edge, whole), (whole, count))
     rows = HALF * (own + 1)
-    edge, whole = lax.div(rows, CHUNK), lax.div(rows + CHUNK - 1, CHUNK)
-    diag = lax.div(HALF * (BLOCKS - 1 - own), CHUNK)
+    edge, whole = lax.div(rows, size), lax.div(rows + size - 1, size)
+    diag = lax.div(HALF * (BLOCKS - 1 - own), size)
     return ((edge, whole), (0, edge)), ((diag, diag + 1), (diag + 1, count))
 
 
-def seen(source, chunk, side, own):
-    row = chunk * CHUNK + lax.broadcasted_iota(jnp.int32, (CHUNK, LANES), 0)
+def seen(source, first, side, own, shape, keys):
+    row = first + lax.broadcasted_iota(jnp.int32, shape, keys)
     block, place = row // HALF, row % HALF
     if source == 0:
         key = block * (2 * HALF) + place
     else:
         key = (BLOCKS - 1 - block) * (2 * HALF) + HALF + place
-    col = lax.broadcasted_iota(jnp.int32, (CHUNK, LANES), 1)
+    col = lax.broadcasted_iota(jnp.int32, shape, 1 - keys)
     return key <= own * (2 * HALF) + side * HALF + col % HALF
 
 
@@ -464,51 +465,35 @@
     return lax.axis_index("ctx") * 2 + lax.axis_index("fsdp")
 
 
-def attend_kernel(kv_ref, q_ref, o_ref, lse_ref, *acc_refs):
+def attend_kernel(kv_ref, q_ref, o_ref, lse_ref, acc_ref):
     me = my_block()
+    lanes = range(0, CHUNK, 128)
     for side in range(2):
         own = me if side == 0 else BLOCKS - 1 - me
         q = q_ref[0, side]
-        for acc in acc_refs:
-            acc[...] = jnp.zeros_like(acc)
-        low = jnp.full((1, LANES), NEGATIVE, jnp.float32)
-        none = jnp.zeros((1, LANES), jnp.float32)
-
-        def step(source, masked, width, first, chunk, carry):
-            out = []
-            for u in range(width):
-                peak, total = carry[u]
-                at = first + (chunk - first) * width + u
-                kv = kv_ref[source, pl.ds(pl.multiple_of(at * CHUNK, CHUNK), CHUNK), :]
-                s = dot_nt(kv, q) * LOG2E
-                if masked:
-                    s = jnp.where(seen(source, at, side, own), s, NEGATIVE)
-                new = jnp.maximum(peak, jnp.max(s, 0, keepdims=True))
-                p = jnp.exp2(s - new)
-                scale = jnp.exp2(peak - new)
-                total = total * scale + jnp.sum(p, 0, keepdims=True)
-                acc_refs[u][...] = acc_refs[u][...] * scale + dot_tn(kv, p.astype(jnp.bfloat16))
-                out.append((new, total))
-            return tuple(out) + tuple(carry[width:])
-
-        carry = ((low, none),) * len(acc_refs)
-        for source, (edge, whole) in enumerate(chunk_ranges(side, own)):
-            carry = lax.fori_loop(edge[0], edge[1], functools.partial(step, source, True, 1, edge[0]), carry)
-            start, end = whole
-            for width in (UNROLL, 1):
-                count = lax.div(end - start, width)
-                carry = lax.fori_loop(
-                    start, start + count, functools.partial(step, source, False, width, start), carry
-                )
-                start = start + count * width
-        peak = functools.reduce(jnp.maximum, [c[0] for c in carry])
-        total, out = none, 0.0
-        for (top, part), acc in zip(carry, acc_refs):
-            scale = jnp.exp2(top - peak)
-            total = total + part * scale
-            out = out + acc[HEAD_SIZE:, :] * scale
-        o_ref[0, side] = out / total
-        lse_ref[0, side] = peak + jnp.log2(total)
+        acc_ref[...] = jnp.zeros_like(acc_ref)
+
+        def step(source, masked, chunk, carry):
+            peak, total = carry
+            kv = kv_ref[source, pl.ds(pl.multiple_of(chunk * CHUNK, CHUNK), CHUNK), :]
+            s = dot_nt(q, kv) * LOG2E
+            if masked:
+                s = jnp.where(seen(source, chunk * CHUNK, side, own, (LANES, CHUNK), 1), s, NEGATIVE)
+            tops = functools.reduce(jnp.maximum, [s[:, k : k + 128] for k in lanes])
+            new = jnp.maximum(peak, jnp.max(tops, 1, keepdims=True))
+            p = jnp.exp2(s - new)
+            scale = jnp.exp2(peak - new)
+            total = total * scale + sum(p[:, k : k + 128] for k in lanes)
+            acc_ref[...] = acc_ref[...] * scale + dot_nn(p.astype(jnp.bfloat16), kv)
+            return new, total
+
+        carry = (jnp.full((LANES, 1), NEGATIVE, jnp.float32), jnp.zeros((LANES, 128), jnp.float32))
+        for source, (edge, whole) in enumerate(chunk_ranges(side, own, CHUNK)):
+            carry = lax.fori_loop(edge[0], edge[1], functools.partial(step, source, True), carry)
+            carry = lax.fori_loop(whole[0], whole[1], functools.partial(step, source, False), carry)
+        peak, total = carry[0], jnp.sum(carry[1], 1, keepdims=True)
+        o_ref[0, side] = (acc_ref[...] / total).T[HEAD_SIZE:, :]
+        lse_ref[0, side] = jnp.broadcast_to(peak + jnp.log2(total), (LANES, 128)).T[:1, :]
 
 
 def attend(kv, q):
@@ -527,7 +512,7 @@
             pl.BlockSpec((1, 2, HEAD_SIZE, LANES), lambda h: (h, 0, 0, 0)),
             pl.BlockSpec((1, 2, 1, LANES), lambda h: (h, 0, 0, 0)),
         ),
-        scratch_shapes=[pltpu.VMEM((128, LANES), jnp.float32)] * UNROLL,
+        scratch_shapes=[pltpu.VMEM((LANES, 128), jnp.float32)],
         compiler_params=pltpu.CompilerParams(vmem_limit_bytes=VMEM_LIMIT),
         name="attend",
     )(kv, q)
@@ -546,11 +531,11 @@
             dq = 0.0
             for u in range(width):
                 at = first + (chunk - first) * width + u
-                rows = pl.ds(pl.multiple_of(at * CHUNK, CHUNK), CHUNK)
+                rows = pl.ds(pl.multiple_of(at * BACK_CHUNK, BACK_CHUNK), BACK_CHUNK)
                 kv = kv_ref[source, rows, :]
                 p = jnp.exp2(dot_nt(kv, q) * LOG2E - lse)
                 if masked:
-                    p = jnp.where(seen(source, at, side, own), p, 0.0)
+                    p = jnp.where(seen(source, at * BACK_CHUNK, side, own, (BACK_CHUNK, LANES), 0), p, 0.0)
                 ds = (p * (dot_nt(kv, do) - delta)).astype(jnp.bfloat16)
                 more = dot_nn(ds, q) + dot_nn(p.astype(jnp.bfloat16), do)
                 dkv_ref[source, rows, :] = (dkv_ref[source, rows, :].astype(jnp.float32) + more).astype(jnp.bfloat16)
@@ -558,7 +543,7 @@
             acc_ref[...] += dq
             return carry
 
-        for source, (edge, whole) in enumerate(chunk_ranges(side, own)):
+        for source, (edge, whole) in enumerate(chunk_ranges(side, own, BACK_CHUNK)):
             lax.fori_loop(edge[0], edge[1], functools.partial(step, source, True, 1, edge[0]), 0)
             start, end = whole
             for width in (UNROLL, 1):
@@ -874,9 +859,9 @@
     slot = lax.broadcasted_iota(jnp.int32, (64, 1024), 0) * 16 + 15
     slot = (slot == lax.broadcasted_iota(jnp.int32, (64, 1024), 1)).astype(bf)
     left = jnp.concatenate([normed, attn_wide, slot], 0)
-    terms = [outer(normed_two, gate_low, 2), outer(normed_two, up_low, 2), outer(left, right, 2)]
+    terms = [outer(normed_two, gate_low, 1), outer(normed_two, up_low, 1), outer(left, right, 1)]
     terms = [a.reshape(2, 2, 4, 4, 2, 16, 1280) for a in terms]
-    terms.append(outer(inner, dy_halves, 3).reshape(2, 2, 4, 4, 2, 48, 512))
+    terms.append(outer(inner, dy_halves, 1).reshape(2, 2, 4, 4, 2, 48, 512))
     parts = tuple(((k, (0, 1280), 0, ALL), (3, (0, 512), 1280, pl.ds(16 * k, 16))) for k in range(3))
     sums, input_grad = scatter(terms, W_DIMS, parts, 16, "scatter_weights", 4, VMEM_LIMIT, (input_grad,))
     down_sum = jnp.concatenate([sums[:, 1280:1792], sums[:, 3072:3584], sums[:, 4864:5376]], 0)

time: 611 us -> 552 us (0.903)
  Pallas kernels: 523 us -> 464 us
    pallas_call x1, Pallas kernels: 88.8 us -> 43.1 us  [attend(): pl.pallas_call(attend_kernel, grid=(KEY_HEADS,), out_shape=(jax.ShapeDtyp...]
    pallas_call x1, Pallas kernels: 84.4 us -> 73.4 us  [attend_back(): pl.pallas_call(attend_back_kernel, grid=(KEY_HEADS,), out_shape=(jax.Shap...]
where the time goes in v3:
time: 552 us; the launch traced here: 543 us
  Pallas kernels  464 us (84%)
  local copies, waits for them, and re-layouts  38.4 us (7%)
  other arithmetic  22.2 us (4%)
  matrix products  16.5 us (3%)
    pallas_call x2, Pallas kernels, scatter(): pl.pallas_call(functools.partial(scatter_kernel, dims, parts, len(ins), l...  155 us
    pallas_call x2, Pallas kernels, gather(): pl.pallas_call(functools.partial(gather_kernel, dims, parts, len(trades))...  150 us
    pallas_call x1, Pallas kernels, attend_back(): pl.pallas_call(attend_back_kernel, grid=(KEY_HEADS,), out_shape=(jax.Shap...  73.4 us
    pallas_call x1, Pallas kernels, attend(): pl.pallas_call(attend_kernel, grid=(KEY_HEADS,), out_shape=(jax.ShapeDtyp...  43.1 us
    pallas_call x1, Pallas kernels, ffn(): pl.pallas_call(ffn_kernel, out_shape=tuple((jax.ShapeDtypeStruct(s, d) fo...  22.8 us
    pallas_call x4, Pallas kernels, outer(): pl.pallas_call(outer_kernel, grid=(2, steps), out_shape=jax.ShapeDtypeStr...  19.8 us
    dot_general x6, matrix products, mm(): return jnp.einsum(form, left, right, preferred_element_type=jnp.float32)  16.5 us

profile of v3, /device:TPU:0, one launch (start us, length us, event | category | flops | bytes accessed | tf_op | source)
XLA Modules:
  0.0 543.3 jit_solution(12143603669988977256)
XLA Ops:
  4.6 0.8 concatenate.70
  5.5 1.9 copy.70.refs_1_
  7.3 1.8 copy.71.refs_2_
  9.1 78.8 %gather_weights.1 = (bf16[2,2,4,4,2,16,5376]{6,5,4,3,2,1,0:T(8,128)(2,1)}, bf16[128,960]{1,0:T(8,128)(2,1)}, bf16[128,960]{1,0:T(8,128)(2,1)}) custom-call(bf16[16,5376]{1,0:T(8,128)(2,1)} %copy-done.5, bf16[128,960]{1,0:T(8,128)(2,1)} %copy.70.refs_1_, bf16[128,960]{1,0:T(8,128)(2,1)} %copy.71.refs_2_), custom_call_target="tpu_custom_call" | custom-call | tf_op jit(solution)/shard_map/gather_weights/pallas_call | solution.py:168
  87.9 1.9 slice_bitcast_fusion.11
  89.9 1.8 multiply_reduce_fusion.3
  92.2 1.0 fusion.48
  94.2 5.5 %fusion.12 = f32[128,2,800]{0,2,1:T(8,128)S(1)} fusion(bf16[2,1024,5376]{2,1,0:T(8,128)(2,1)} %bitcast.103, bf16[128,1024]{1,0:T(8,128)(2,1)S(1)} %multiply_convert_fusion), kind=kOutput, calls=%fused_computation.19 | convolution fusion | flops 419430400 | bytes 4751360 | tf_op jit(solution)/shard_map/te,hec->thc/dot_general | solution.py:594
  100.9 1.1 copy.81
  102.0 0.9 pad.61.q_ref
  104.9 0.9 reshape.339.refs_0_
  105.8 71.1 %gather_keys.1 = bf16[2,2,4,4,2,2,64,640]{7,6,5,4,3,2,1,0:T(8,128)(2,1)} custom-call(bf16[2,64,640]{2,1,0:T(8,128)(2,1)} %reshape.339.refs_0_), custom_call_target="tpu_custom_call" | custom-call | tf_op jit(solution)/shard_map/gather_keys/pallas_call | solution.py:168
  176.9 43.1 %attend.1 = (f32[5,2,64,192]{3,2,1,0:T(8,128)}, f32[5,2,1,192]{3,2,1,0:T(1,128)}) custom-call(bf16[2,8192,640]{2,1,0:T(8,128)(2,1)} %bitcast.99, bf16[5,2,192,128]{3,2,1,0:T(8,128)(2,1)} %pad.61.q_ref), custom_call_target="tpu_custom_call" | custom-call | tf_op jit(solution)/shard_map/attend/pallas_call | solution.py:500
  220.0 1.4 copy.82
  222.8 0.8 select_maximum_fusion.attn_ref
  223.6 1.7 fusion.40.x_ref
  225.4 1.6 fusion.41.dy_ref.right_ref
  227.0 1.0 fusion.47
  228.9 3.5 fusion.27.spread_ref
  232.4 2.4 fusion.16.spread_down_ref
  234.8 22.8 %ffn.1 = (bf16[2,128,512]{2,1,0:T(8,128)(2,1)}, f32[2,128,512]{2,1,0:T(8,128)}, bf16[2,128,512]{2,1,0:T(8,128)(2,1)}, bf16[128,1024]{1,0:T(8,128)(2,1)}, bf16[12...) custom-call(bf16[2,64,16,5376]{3,2,1,0:T(8,128)(2,1)} %bitcast.105, ...), custom_call_target="tpu_custom_call" | custom-call | tf_op jit(solution)/shard_map/ffn/pallas_call | solution.py:735
  257.6 1.0 slice_bitcast_fusion.9
  259.2 1.1 copy.88
  261.3 1.1 copy.87
  262.3 1.0 pad.65.do_ref
  263.4 73.4 %attend_back.1 = (f32[5,2,64,192]{3,2,1,0:T(8,128)}, bf16[2,8192,640]{2,1,0:T(8,128)(2,1)}) custom-call(bf16[2,8192,640]{2,1,0:T(8,128)(2,1)} %bitcast.100, bf16[5,2,192,128]{3,2,1,0:T(8,128)(2,1)} %pad.61.q_ref, bf16[5,2,192,128]{3,2,1,0:T(8,128)(2,1)} %pad.65.do_ref, f32[5,2,1,192]{3,2,1,0:T(1,128)} %get-tuple-element.73.lse_ref, ...), custom_call_target="tpu_custom_call" | custom-call | tf_op jit(solution)/shard_map/attend_back/pallas_call | solution.py:560
  336.8 1.2 broadcast_multiply_fusion
  338.3 1.2 copy.91
  341.2 86.1 %scatter_keys.1 = (f32[2,64,640]{2,1,0:T(8,128)}, bf16[128,960]{1,0:T(8,128)(2,1)}) custom-call(bf16[2,2,4,4,2,2,64,640]{7,6,5,4,3,2,1,0:T(8,128)(2,1)} %bitcast.108, bf16[128,960]{1,0:T(8,128)(2,1)} %pad_maximum_fusion.4.refs_1_), custom_call_target="tpu_custom_call" | custom-call | tf_op jit(solution)/shard_map/scatter_keys/pallas_call | solution.py:388
  427.4 1.0 reshape.350
  429.8 3.9 multiply_reduce_fusion.1
  433.9 1.8 fusion.25
  435.7 1.8 convolution_add_fusion.1
  437.5 1.8 fusion.19
  439.4 1.1 maximum_add_fusion.refs_4_
  440.4 5.2 outer.7
  446.2 1.5 fusion.18.right_ref
  447.8 0.9 pad_maximum_fusion.left_ref
  448.7 6.0 %outer.6 = bf16[2,1024,1280]{2,1,0:T(8,128)(2,1)} custom-call(bf16[320,1024]{1,0:T(8,128)(2,1)} %pad_maximum_fusion.left_ref, bf16[2,320,1280]{2,1,0:T(8,128)(2,1)} %fusion.18.right_ref), custom_call_target="tpu_custom_call" | custom-call | tf_op jit(solution)/shard_map/outer/pallas_call | solution.py:614
  454.6 4.3 outer.5
  458.9 4.4 outer.4
  463.3 69.3 %scatter_weights.1 = (f32[16,5376]{1,0:T(8,128)}, f32[128,960]{1,0:T(8,128)}) custom-call(bf16[2,2,4,4,2,16,1280]{6,5,4,3,2,1,0:T(8,128)(2,1)} %bitcast.110, bf16[2,2,4,4,2,16,1280]{6,5,4,3,2,1,0:T(8,128)(2,1)} %bitcast.109, bf16[2,2,4,4,2,16,1280]{6,5,4,3,2,1,0:T(8,128)(2,1)} %bitcast.107, bf16[2,2,4,4,2,48,512]{6,5,4,3,2,1,0:T(8,128)(2,1)} %bitcast.101, ...), custom_call_target="tpu_custom_call" | custom-call | tf_op jit(solution)/shard_map/scatter_weights/pallas_call | solution.py:388
  534.0 2.0 copy.104
  536.1 1.6 fusion.80
  537.6 1.5 fusion.81
  539.2 1.5 fusion.82
  540.7 1.3 slice_bitcast_fusion.18
  542.0 0.8 copy.103
  (124 shorter events, 17.9 us)
Async XLA Ops:
  5.5 3.7 copy-start.5
  89.8 1.9 copy-start.3
  89.8 1.9 copy-start.4
  89.8 1.9 copy-start.17
  89.9 1.9 copy-start.19
  92.2 8.7 %copy-start.14 = (f32[128]{0:T(128)}, f32[128]{0:T(128)S(1)}, u32[]{:S(2)}) copy-start(f32[128]{0:T(128)S(1)} %get-tuple-element.167) | copy-start | bytes 1540
  93.3 7.6 %copy-start.11 = (f32[1024]{0:T(1024)}, f32[1024]{0:T(1024)S(1)}, u32[]{:S(2)}) copy-start(f32[1024]{0:T(1024)S(1)} %reshape.355) | copy-start | bytes 12292
  93.4 0.7 copy-start
  336.7 3.4 copy-start.10
  336.8 3.6 copy-start.9
  427.3 2.4 copy-start.12
  427.4 2.4 copy-start.15
  429.1 4.6 copy-start.16
  429.7 4.1 copy-start.18
  429.8 4.1 copy-start.20
  437.4 1.8 copy-start.2
  439.3 6.3 %copy-start.13 = (f32[2,1,512]{2,1,0:T(1,128)S(1)}, f32[2,1,512]{2,1,0:T(1,128)}, u32[]{:S(2)}) copy-start(f32[2,1,512]{2,1,0:T(1,128)} %get-tuple-element.84) | copy-start | bytes 12292
  440.4 5.8 %copy-start.7 = (bf16[2,128,512]{2,1,0:T(8,128)(2,1)S(1)}, bf16[2,128,512]{2,1,0:T(8,128)(2,1)}, u32[]{:S(2)}) copy-start(bf16[2,128,512]{2,1,0:T(8,128)(2,1)} %get-tuple-element.83) | copy-start | bytes 786436
  440.4 7.4 %copy-start.1 = (bf16[128,1024]{1,0:T(8,128)(2,1)S(1)}, bf16[128,1024]{1,0:T(8,128)(2,1)}, u32[]{:S(2)}) copy-start(bf16[128,1024]{1,0:T(8,128)(2,1)} %copy-done) | copy-start | bytes 786436
  440.4 7.4 %copy-start.6 = (bf16[128,1024]{1,0:T(8,128)(2,1)S(1)}, bf16[128,1024]{1,0:T(8,128)(2,1)}, u32[]{:S(2)}) copy-start(bf16[128,1024]{1,0:T(8,128)(2,1)} %get-tuple-element.80) | copy-start | bytes 786436
  463.3 78.7 %copy-start.8 = (bf16[128,960]{1,0:T(8,128)(2,1)S(1)}, bf16[128,960]{1,0:T(8,128)(2,1)}, u32[]{:S(2)}) copy-start(bf16[128,960]{1,0:T(8,128)(2,1)} %get-tuple-element.111) | copy-start | bytes 737284

commit v4 on v3

--- a/solution.py
+++ b/solution.py
@@ -402,7 +402,8 @@
 
 
 W_DIMS = ("zl", "zh", "x", "y", "c")
-W_PARTS = ((0, 1792), (1792, 1792), (3584, 1792))
+FIRST_PARTS = ((0, 512), (512, 512), (1024, 256))
+REST_PARTS = ((0, 1280), (1280, 1280), (2560, 1536))
 T_DIMS = ("l", "zh", "x", "y", "c", "zl")
 T_PARTS = ((0, 256), (256, 256), (512, 128))
 
@@ -465,10 +466,96 @@
     return lax.axis_index("ctx") * 2 + lax.axis_index("fsdp")
 
 
-def attend_kernel(kv_ref, q_ref, o_ref, lse_ref, acc_ref):
+def gather_steps(dims, parts, piece_ref, out_ref, sems):
+    send, recv, sib_send, sib_recv, own_sem = sems
+    me = whereabouts()
+    sibling = device_at(moved(me, "c", 1))
+    rings, sibs = {}, {}
+    for i, cols in enumerate(parts):
+        for phase in range(3):
+            axis = ORDERS[i][phase]
+            base = dict(me)
+            for done in ORDERS[i][:phase]:
+                base[done] = ALL
+
+            def blk(by, half=None, base=base, axis=axis, cols=cols):
+                at = {**base, axis: lax.rem(me[axis] + by + 4, 4)}
+                return view(out_ref, dims, at, cols, half)
+
+            right, left = device_at(moved(me, axis, 1)), device_at(moved(me, axis, -1))
+            moves = ((blk(0), right), (blk(0), left), (blk(-1, 0), right), (blk(1, 1), left))
+            rings[i, phase] = [
+                pltpu.make_async_remote_copy(
+                    src_ref=ref,
+                    dst_ref=ref,
+                    send_sem=send.at[i, phase, k],
+                    recv_sem=recv.at[i, phase, k],
+                    device_id=to,
+                    device_id_type=MESH,
+                )
+                for k, (ref, to) in enumerate(moves)
+            ]
+            if phase == 2:
+                sibs[i] = [
+                    pltpu.make_async_remote_copy(
+                        src_ref=blk(by),
+                        dst_ref=blk(by),
+                        send_sem=sib_send.at[i, k],
+                        recv_sem=sib_recv.at[i, k],
+                        device_id=sibling,
+                        device_id_type=MESH,
+                    )
+                    for k, by in enumerate((0, -1, 1, 2))
+                ]
+    own = pltpu.make_async_copy(piece_ref, out_ref.at[tuple(place(dims, me)) + (ALL, ALL)], own_sem)
+    count = range(len(parts))
+
+    def step(k):
+        phase = k // 2
+        if k == 0:
+            greet(me)
+            own.start()
+            own.wait()
+        if k % 2 == 0:
+            for i in count:
+                if 0 < phase:
+                    rings[i, phase - 1][2].wait_recv()
+                    rings[i, phase - 1][3].wait_recv()
+                if phase < 3:
+                    rings[i, phase][0].start()
+                    rings[i, phase][1].start()
+                if phase == 2:
+                    sibs[i][0].start()
+                if phase == 3:
+                    sibs[i][3].start()
+        elif phase < 3:
+            for i in count:
+                for side in range(2):
+                    rings[i, phase][side].wait_recv()
+                    rings[i, phase][2 + side].start()
+                    if phase == 2:
+                        sibs[i][1 + side].start()
+        else:
+            for i in count:
+                for c in sibs[i]:
+                    c.wait_recv()
+                    c.wait_send()
+                for phase in range(3):
+                    for c in rings[i, phase]:
+                        c.wait_send()
+
+    return step
+
+
+def attend_kernel(kv_ref, q_ref, piece_ref, o_ref, lse_ref, rest_ref, acc_ref, *sems):
     me = my_block()
+    head = pl.program_id(0)
+    transfer = gather_steps(W_DIMS, REST_PARTS, piece_ref, rest_ref, sems)
     lanes = range(0, CHUNK, 128)
     for side in range(2):
+        for turn in range(KEY_HEADS - 1):
+            if 2 * turn + side < 7:
+                pl.when(head == turn)(functools.partial(transfer, 2 * turn + side))
         own = me if side == 0 else BLOCKS - 1 - me
         q = q_ref[0, side]
         acc_ref[...] = jnp.zeros_like(acc_ref)
@@ -494,28 +581,42 @@
         peak, total = carry[0], jnp.sum(carry[1], 1, keepdims=True)
         o_ref[0, side] = (acc_ref[...] / total).T[HEAD_SIZE:, :]
         lse_ref[0, side] = jnp.broadcast_to(peak + jnp.log2(total), (LANES, 128)).T[:1, :]
-
-
-def attend(kv, q):
+    pl.when(head == KEY_HEADS - 1)(functools.partial(transfer, 7))
+
+
+def attend(kv, q, piece):
+    n = len(REST_PARTS)
     return pl.pallas_call(
         attend_kernel,
         grid=(KEY_HEADS,),
         out_shape=(
             jax.ShapeDtypeStruct((KEY_HEADS, 2, HEAD_SIZE, LANES), jnp.float32),
             jax.ShapeDtypeStruct((KEY_HEADS, 2, 1, LANES), jnp.float32),
+            jax.ShapeDtypeStruct((2, 2, 4, 4, 2) + piece.shape, piece.dtype),
         ),
         in_specs=[
             pl.BlockSpec((2, SIDE, 128), lambda h: (0, 0, h)),
             pl.BlockSpec((1, 2, LANES, 128), lambda h: (h, 0, 0, 0)),
+            pl.BlockSpec(memory_space=pl.ANY),
         ],
         out_specs=(
             pl.BlockSpec((1, 2, HEAD_SIZE, LANES), lambda h: (h, 0, 0, 0)),
             pl.BlockSpec((1, 2, 1, LANES), lambda h: (h, 0, 0, 0)),
+            pl.BlockSpec(memory_space=pl.ANY),
         ),
-        scratch_shapes=[pltpu.VMEM((LANES, 128), jnp.float32)],
-        compiler_params=pltpu.CompilerParams(vmem_limit_bytes=VMEM_LIMIT),
+        scratch_shapes=[
+            pltpu.VMEM((LANES, 128), jnp.float32),
+            pltpu.SemaphoreType.DMA((n, 3, 4)),
+            pltpu.SemaphoreType.DMA((n, 3, 4)),
+            pltpu.SemaphoreType.DMA((n, 4)),
+            pltpu.SemaphoreType.DMA((n, 4)),
+            pltpu.SemaphoreType.DMA,
+        ],
+        compiler_params=pltpu.CompilerParams(
+            collective_id=5, has_side_effects=True, vmem_limit_bytes=VMEM_LIMIT
+        ),
         name="attend",
-    )(kv, q)
+    )(kv, q, piece)
 
 
 def attend_back_kernel(kv_ref, q_ref, do_ref, lse_ref, delta_ref, dq_ref, dkv_ref, acc_ref):
@@ -633,23 +734,24 @@
 
 
 def ffn_kernel(
-    whole_ref, attn_ref, x_ref, dy_ref, gain_ref, spread_ref, spread_down_ref,
+    first_ref, rest_ref, attn_ref, x_ref, dy_ref, gain_ref, spread_ref, spread_down_ref,
     layer_out_ref, middle_grad_ref, attn_grad_ref, attn_wide_ref, normed_ref, gate_low_ref, up_low_ref,
     inner_ref, middle_low_ref, gain_grad_ref,
     w_out, w_gate, w_up, w_down, gate_s, up_s, sems,
 ):
     bf, f32 = jnp.bfloat16, jnp.float32
 
-    def fetch(dst, start, width, sem):
-        c = pltpu.make_async_copy(whole_ref.at[:, :, :, pl.ds(start, width)], dst, sem)
+    def fetch(dst, src, start, width, sem):
+        c = pltpu.make_async_copy(src.at[:, :, :, pl.ds(start, width)], dst, sem)
         c.start()
         return c
 
-    get_out = fetch(w_out, 3584, 512, sems.at[0])
-    get_gate = fetch(w_gate, 0, 1280, sems.at[1])
-    get_up = fetch(w_up, 1792, 1280, sems.at[2])
+    get_out = fetch(w_out, first_ref, 0, 512, sems.at[0])
+    get_gate = fetch(w_gate, rest_ref, 0, 1280, sems.at[1])
+    get_up = fetch(w_up, rest_ref, 1280, 1280, sems.at[2])
     get_down = [
-        fetch(w_down.at[:, :, pl.ds(16 * g, 16), :], 1280 + 1792 * g, 512, sems.at[3 + g]) for g in range(3)
+        fetch(w_down.at[:, :, pl.ds(16 * g, 16), :], rest_ref, 2560 + 512 * g, 512, sems.at[3 + g])
+        for g in range(3)
     ]
     real = lax.broadcasted_iota(jnp.int32, (128, 512), 1) < 480
 
@@ -725,7 +827,7 @@
         attn_grad_ref[h] = dot_nt(wide_grad, spread_ref[h]).astype(bf)
 
 
-def ffn(whole, attn, x, dy, gain, spread, spread_down):
+def ffn(first, rest, attn, x, dy, gain, spread, spread_down):
     bf, f32 = jnp.bfloat16, jnp.float32
     vmem = pl.BlockSpec(memory_space=pltpu.VMEM)
     shapes = [
@@ -735,7 +837,7 @@
     return pl.pallas_call(
         ffn_kernel,
         out_shape=tuple(jax.ShapeDtypeStruct(s, d) for s, d in shapes),
-        in_specs=[pl.BlockSpec(memory_space=pl.ANY)] + [vmem] * 6,
+        in_specs=[pl.BlockSpec(memory_space=pl.ANY)] * 2 + [vmem] * 6,
         out_specs=(vmem,) * len(shapes),
         scratch_shapes=[
             pltpu.VMEM((2, 64, 16, 512), bf),
@@ -748,7 +850,7 @@
         ],
         compiler_params=pltpu.CompilerParams(vmem_limit_bytes=VMEM_LIMIT),
         name="ffn",
-    )(whole, attn, x, dy, gain, spread, spread_down)
+    )(first, rest, attn, x, dy, gain, spread, spread_down)
 
 
 def halves(rows):
@@ -776,18 +878,18 @@
     bf, f32 = jnp.bfloat16, jnp.float32
     me = my_block()
 
-    down = jnp.zeros((48, 512), bf)
-    down = down.at[:40, :480].set(down_weight)
-    down = down.at[40, :15].set(attn_gain).at[41, :15].set(ffn_gain)
-    down = down.reshape(3, 16, 512)
+    gains = jnp.pad(jnp.concatenate([attn_gain, ffn_gain])[None], ((0, 0), (0, 1250)))
     oqkv = jnp.concatenate([output_weight, query_weight, key_weight, value_weight], 1)
-    mats = [jnp.pad(a, ((0, 1), (0, 0))) for a in (gate_weight, up_weight, oqkv)]
-    piece = jnp.concatenate([a for i in range(3) for a in (mats[i], down[i])], 1)
-    whole, x_low, dy = gather(piece, W_DIMS, W_PARTS, "gather_weights", 1, (layer_in, out_cotangent))
-    whole = whole.reshape(2, 64, 16, 5376)
-    w_qkv = whole.reshape(2, 1024, 5376)[:, :, 4064:4864]
-    gain_one = whole[0, :, 8, 4864:4880].reshape(1024).astype(f32)
-    gain_two = whole[0, :, 9, 4864:4879].reshape(1, 960).astype(f32)
+    first, x_low, dy = gather(
+        jnp.concatenate([oqkv, gains], 0), W_DIMS, FIRST_PARTS, "gather_first", 1, (layer_in, out_cotangent)
+    )
+    first = first.reshape(2, 64, 16, 1280)
+    w_qkv = first.reshape(2, 1024, 1280)[:, :, 480:]
+    gain_one = jnp.pad(first[0, :, 15, :15], ((0, 0), (0, 1))).reshape(1024).astype(f32)
+    gain_two = first[0, :, 15, 15:30].reshape(1, 960).astype(f32)
+    down = jnp.pad(down_weight, ((0, 8), (0, 32))).reshape(3, 16, 512)
+    wide = jnp.pad(jnp.concatenate([gate_weight, up_weight], 1), ((0, 1), (0, 0)))
+    rest = jnp.concatenate([wide, down[0], down[1], down[2]], 1)
 
     i = lax.broadcasted_iota(jnp.int32, (2, 512, 1024), 1)
     d = i + 480 * lax.broadcasted_iota(jnp.int32, (2, 512, 1024), 0)
@@ -817,10 +919,11 @@
     (kv,) = gather(kv_piece, T_DIMS, T_PARTS, "gather_keys", 2)
     kv = kv.reshape(2, SIDE, 640)
     q_heads = jnp.pad(by_head(query_rot * jnp.asarray(0.125, bf)), ((0, 0), (0, 0), (0, 0), (0, 64)))
-    attn_heads, lse = attend(kv, q_heads)
+    attn_heads, lse, rest = attend(kv, q_heads, rest)
+    rest = rest.reshape(2, 64, 16, 4096)
     attn = by_token(attn_heads)
     (layer_out, middle_grad, attn_grad, attn_wide, normed_two, gate_low, up_low, inner, middle_low, gain_two_term) = ffn(
-        whole, halves(attn), x_halves, dy_halves, halves(gain_two), spread, spread_down
+        first, rest, halves(attn), x_halves, dy_halves, halves(gain_two), spread, spread_down
     )
     layer_out, middle_grad, attn_grad = joined(layer_out), joined(middle_grad), joined(attn_grad)
     delta = jnp.sum((attn_grad.astype(f32) * attn).reshape(2, HALF, KEY_HEADS, GROUPS, HEAD_SIZE), -1)

time: 552 us -> 552 us (level)
    pallas_call x1, Pallas kernels: 43.1 us -> 81.5 us  [attend(): pl.pallas_call(attend_kernel, grid=(KEY_HEADS,), out_shape=(jax.ShapeDtyp...]
    pallas_call x2, Pallas kernels: 150 us -> 120 us  [gather(): pl.pallas_call(functools.partial(gather_kernel, dims, parts, len(trades))...]
where the time goes in v4:
time: 552 us; the launch traced here: 544 us
  Pallas kernels  467 us (85%)
  local copies, waits for them, and re-layouts  35 us (6%)
  other arithmetic  23.4 us (4%)
  matrix products  16.3 us (3%)
    pallas_call x2, Pallas kernels, scatter(): pl.pallas_call(functools.partial(scatter_kernel, dims, parts, len(ins), l...  150 us
    pallas_call x2, Pallas kernels, gather(): pl.pallas_call(functools.partial(gather_kernel, dims, parts, len(trades))...  120 us
    pallas_call x1, Pallas kernels, attend(): pl.pallas_call(attend_kernel, grid=(KEY_HEADS,), out_shape=(jax.ShapeDtyp...  81.5 us
    pallas_call x1, Pallas kernels, attend_back(): pl.pallas_call(attend_back_kernel, grid=(KEY_HEADS,), out_shape=(jax.Shap...  73.4 us
    pallas_call x1, Pallas kernels, ffn(): pl.pallas_call(ffn_kernel, out_shape=tuple((jax.ShapeDtypeStruct(s, d) fo...  22.8 us
    pallas_call x4, Pallas kernels, outer(): pl.pallas_call(outer_kernel, grid=(2, steps), out_shape=jax.ShapeDtypeStr...  19.7 us
    dot_general x6, matrix products, mm(): return jnp.einsum(form, left, right, preferred_element_type=jnp.float32)  16.3 us

profile of v4, /device:TPU:0, one launch (start us, length us, event | category | flops | bytes accessed | tf_op | source)
XLA Modules:
  0.0 544.0 jit_solution(8858843914342925653)
XLA Ops:
  0.6 1.8 copy.72.refs_1_
  2.4 1.8 copy.73.refs_2_
  4.2 0.8 concatenate.73
  6.4 49.2 %gather_first.1 = (bf16[2,2,4,4,2,16,1280]{6,5,4,3,2,1,0:T(8,128)(2,1)}, bf16[128,960]{1,0:T(8,128)(2,1)}, bf16[128,960]{1,0:T(8,128)(2,1)}) custom-call(bf16[16,1280]{1,0:T(8,128)(2,1)} %fusion.51.refs_0_, bf16[128,960]{1,0:T(8,128)(2,1)} %copy.72.refs_1_, bf16[128,960]{1,0:T(8,128)(2,1)} %copy.73.refs_2_), custom_call_target="tpu_custom_call" | custom-call | tf_op jit(solution)/shard_map/gather_first/pallas_call | solution.py:168
  55.6 1.9 slice_bitcast_fusion.11
  57.6 1.8 multiply_reduce_fusion.3
  60.0 0.9 slice.211
  61.3 5.4 fusion.12
  69.6 0.9 reshape.252.refs_0_
  70.5 70.5 %gather_keys.1 = bf16[2,2,4,4,2,2,64,640]{7,6,5,4,3,2,1,0:T(8,128)(2,1)} custom-call(bf16[2,64,640]{2,1,0:T(8,128)(2,1)} %reshape.252.refs_0_), custom_call_target="tpu_custom_call" | custom-call | tf_op jit(solution)/shard_map/gather_keys/pallas_call | solution.py:168
  141.4 1.3 copy.85
  142.7 0.9 pad.54.q_ref
  144.3 81.5 %attend.1 = (f32[5,2,64,192]{3,2,1,0:T(8,128)}, f32[5,2,1,192]{3,2,1,0:T(1,128)}, bf16[2,2,4,4,2,16,4096]{6,5,4,3,2,1,0:T(8,128)(2,1)}) custom-call(bf16[2,8192,640]{2,1,0:T(8,128)(2,1)} %bitcast.101, bf16[5,2,192,128]{3,2,1,0:T(8,128)(2,1)} %pad.54.q_ref, bf16[16,4096]{1,0:T(8,128)(2,1)} %pad_maximum_fusion.7.piece_ref), custom_call_target="tpu_custom_call" | custom-call | tf_op jit(solution)/shard_map/attend/pallas_call | solution.py:589
  225.9 1.4 copy.86
  228.7 0.8 select_maximum_fusion.attn_ref
  229.5 1.7 fusion.40.x_ref
  231.3 1.7 fusion.41.dy_ref.right_ref
  232.9 1.1 fusion.52
  234.8 3.5 fusion.27.spread_ref
  238.4 2.5 fusion.16.spread_down_ref
  240.9 22.8 %ffn.1 = (bf16[2,128,512]{2,1,0:T(8,128)(2,1)}, f32[2,128,512]{2,1,0:T(8,128)}, bf16[2,128,512]{2,1,0:T(8,128)(2,1)}, bf16[128,1024]{1,0:T(8,128)(2,1)}, bf16[12...) custom-call(bf16[2,64,16,1280]{3,2,1,0:T(8,128)(2,1)} %bitcast.114, ...), custom_call_target="tpu_custom_call" | custom-call | tf_op jit(solution)/shard_map/ffn/pallas_call | solution.py:837
  263.6 1.0 slice_bitcast_fusion.9
  265.2 1.1 copy.92
  267.3 1.1 copy.91
  268.4 1.0 pad.60.do_ref
  269.4 73.4 %attend_back.1 = (f32[5,2,64,192]{3,2,1,0:T(8,128)}, bf16[2,8192,640]{2,1,0:T(8,128)(2,1)}) custom-call(bf16[2,8192,640]{2,1,0:T(8,128)(2,1)} %bitcast.102, bf16[5,2,192,128]{3,2,1,0:T(8,128)(2,1)} %pad.54.q_ref, bf16[5,2,192,128]{3,2,1,0:T(8,128)(2,1)} %pad.60.do_ref, f32[5,2,1,192]{3,2,1,0:T(1,128)} %get-tuple-element.39.lse_ref, ...), custom_call_target="tpu_custom_call" | custom-call | tf_op jit(solution)/shard_map/attend_back/pallas_call | solution.py:661
  342.8 1.2 broadcast_multiply_fusion
  344.4 1.2 copy.95
  347.3 81.3 %scatter_keys.1 = (f32[2,64,640]{2,1,0:T(8,128)}, bf16[128,960]{1,0:T(8,128)(2,1)}) custom-call(bf16[2,2,4,4,2,2,64,640]{7,6,5,4,3,2,1,0:T(8,128)(2,1)} %bitcast.105, bf16[128,960]{1,0:T(8,128)(2,1)} %pad_maximum_fusion.4.refs_1_), custom_call_target="tpu_custom_call" | custom-call | tf_op jit(solution)/shard_map/scatter_keys/pallas_call | solution.py:388
  428.6 1.0 reshape.264
  431.0 3.7 multiply_reduce_fusion.1
  435.0 1.8 fusion.25
  436.7 1.8 convolution_add_fusion.1
  438.5 1.8 fusion.19
  440.5 1.0 maximum_add_fusion.refs_4_
  442.1 1.4 fusion.18.right_ref
  443.7 0.9 pad_maximum_fusion.left_ref
  444.6 6.2 %outer.6 = bf16[2,1024,1280]{2,1,0:T(8,128)(2,1)} custom-call(bf16[320,1024]{1,0:T(8,128)(2,1)} %pad_maximum_fusion.left_ref, bf16[2,320,1280]{2,1,0:T(8,128)(2,1)} %fusion.18.right_ref), custom_call_target="tpu_custom_call" | custom-call | tf_op jit(solution)/shard_map/outer/pallas_call | solution.py:715
  450.8 4.3 outer.5
  455.0 4.4 outer.4
  459.4 4.9 outer.7
  464.3 69.0 %scatter_weights.1 = (f32[16,5376]{1,0:T(8,128)}, f32[128,960]{1,0:T(8,128)}) custom-call(bf16[2,2,4,4,2,16,1280]{6,5,4,3,2,1,0:T(8,128)(2,1)} %bitcast.107, bf16[2,2,4,4,2,16,1280]{6,5,4,3,2,1,0:T(8,128)(2,1)} %bitcast.106, bf16[2,2,4,4,2,16,1280]{6,5,4,3,2,1,0:T(8,128)(2,1)} %bitcast.104, bf16[2,2,4,4,2,48,512]{6,5,4,3,2,1,0:T(8,128)(2,1)} %bitcast.103, ...), custom_call_target="tpu_custom_call" | custom-call | tf_op jit(solution)/shard_map/scatter_weights/pallas_call | solution.py:388
  534.7 2.0 copy.108
  536.7 1.6 fusion.84
  538.3 1.5 fusion.85
  539.9 1.5 fusion.86
  541.4 1.3 slice_bitcast_fusion.18
  542.7 0.8 copy.107
  (127 shorter events, 15.5 us)
Async XLA Ops:
  57.5 1.9 copy-start.3
  57.6 1.9 copy-start.4
  57.6 1.9 copy-start.19
  57.6 1.9 copy-start.21
  60.0 8.2 %copy-start.16 = (f32[128]{0:T(128)}, f32[128]{0:T(128)S(1)}, u32[]{:S(2)}) copy-start(f32[128]{0:T(128)S(1)} %get-tuple-element.136) | copy-start | bytes 1540
  61.2 7.0 %copy-start.13 = (f32[1024]{0:T(1024)}, f32[1024]{0:T(1024)S(1)}, u32[]{:S(2)}) copy-start(f32[1024]{0:T(1024)S(1)} %reshape.269) | copy-start | bytes 12292
  61.3 5.5 %copy-start = (bf16[128,1024]{1,0:T(8,128)(2,1)}, bf16[128,1024]{1,0:T(8,128)(2,1)S(1)}, u32[]{:S(2)}) copy-start(bf16[128,1024]{1,0:T(8,128)(2,1)S(1)} %multiply_convert_fusion) | copy-start | bytes 786436
  140.9 2.7 copy-start.12
  141.0 2.7 copy-start.10
  141.0 2.7 copy-start.11
  342.8 3.4 copy-start.9
  342.8 3.6 copy-start.8
  428.6 2.4 copy-start.14
  428.6 2.4 copy-start.17
  430.4 4.4 copy-start.18
  431.0 3.9 copy-start.20
  431.0 3.9 copy-start.22
  438.5 1.9 copy-start.2
  438.5 3.1 copy-start.15
  440.3 1.8 copy-start.6
  440.3 3.3 copy-start.1
  440.4 3.3 copy-start.5
  464.3 78.4 %copy-start.7 = (bf16[128,960]{1,0:T(8,128)(2,1)S(1)}, bf16[128,960]{1,0:T(8,128)(2,1)}, u32[]{:S(2)}) copy-start(bf16[128,960]{1,0:T(8,128)(2,1)} %get-tuple-element.77) | copy-start | bytes 737284
